TPU v7x, 128 devices: a whole 4x4x4 slice. The times are simulated.
128 devices in a mesh: grp: 4 (over x), dev: 32 (over y, z, core).
Axes of the slice: x: 4, y: 4, z: 4, core: 2. Of those that a mesh axis runs over, the one named last changes fastest.
Arguments:
- strength: bfloat16 [16384, 2, 120, 120], P(('grp', 'dev')), may hold values from -20 to 20
- freqs: float32 [16384, 3, 120], P(('grp', 'dev')), may hold values from 0.6 to 4.6
- owner: int32 [16384, 1], P(('grp', 'dev')), may hold values from 0 to 127; in each aligned block of 128 rows (0 to 127, 128 to 255, ...) at most 2 rows name the same one
- tile_slot: int32 [16384], P(('grp', 'dev')), may hold values from 0 to 127
- live_count: int32 [128], P(('grp', 'dev')), may hold values from 1 to 128, 14336 in all
Outputs:
- collision: float32 [128, 120, 4, 32, 120], P('grp', None, None, 'dev')
Inputs may be any that keep to these rules, and one draw needn't show every extreme that they name: Among the live triplets of one device at most 2 name one owner; some owner is named by exactly 2 rows of some device. `live_count`: some device has all 128 slots live.
All inputs are finite; a program needn't handle non-finite values.
Results may differ from a plain program's by a relative error of at most 0.0046.
Values may be sent and summed in bfloat16 or wider, within the bound.
A program may use at most 128 MiB of HBM per device.

v0:
```python
import jax
import jax.numpy as jnp
from jax import lax
from jax.sharding import PartitionSpec as P


def per_device(strength, freqs, owner, tile_slot, live_count):
    trip = strength.shape[0]
    bands = strength.shape[2]
    n_grp = lax.axis_size("grp")
    n_dev = lax.axis_size("dev")
    devices = n_grp * n_dev
    cap = max(2, (2 * trip + devices - 1) // devices)
    occ = 1.0 / (jnp.exp(freqs) - 1.0)
    rowf = jnp.sqrt(occ[:, 0] * (occ[:, 0] + 1.0))
    colf = jnp.sqrt(occ[:, 1] * (occ[:, 1] + 1.0))
    third = occ[:, 2] + 1.0
    scaled = (strength[:, 0] * third[:, None, :]).astype(jnp.bfloat16)
    core = jnp.einsum("tjk,tlk->tjl", scaled, strength[:, 1], preferred_element_type=jnp.float32)
    diff = freqs[:, 0, :, None] - freqs[:, 1, None, :]
    block = (rowf[:, :, None] * colf[:, None, :] * jnp.exp(-diff * diff / 0.5) * core).astype(
        jnp.bfloat16
    )
    live = jnp.arange(trip, dtype=jnp.int32) < live_count[0]
    target = owner[:, 0]
    same = (target[:, None] == target[None, :]) & live[:, None] & live[None, :]
    before = jnp.sum(jnp.tril(same.astype(jnp.int32), -1), axis=1)
    place = jnp.where(live, target * cap + before, devices * cap)
    tile_order = tile_slot % n_grp * n_dev + tile_slot // n_grp
    outgoing = (
        jnp.zeros((devices * cap, bands, bands), jnp.bfloat16).at[place].set(block, mode="drop")
    )
    labels = jnp.full((devices * cap,), -1, jnp.int32).at[place].set(tile_order, mode="drop")
    got_blocks, got_labels = (
        lax.all_to_all(
            outgoing.reshape(devices, cap, bands, bands),
            ("grp", "dev"),
            split_axis=0,
            concat_axis=0,
            tiled=True,
        ),
        lax.all_to_all(
            labels.reshape(devices, cap), ("grp", "dev"), split_axis=0, concat_axis=0, tiled=True
        ),
    )
    flat_blocks = got_blocks.reshape(devices * cap, bands * bands)
    flat_labels = got_labels.reshape(devices * cap)
    selector = (flat_labels[None, :] == jnp.arange(devices, dtype=jnp.int32)[:, None]).astype(
        jnp.bfloat16
    )
    omega = jnp.dot(selector, flat_blocks, preferred_element_type=jnp.float32)
    rounded = omega.astype(jnp.bfloat16).reshape(n_grp, n_dev, bands, bands)
    partner = lax.all_to_all(
        rounded.reshape(devices, bands, bands),
        ("grp", "dev"),
        split_axis=0,
        concat_axis=0,
        tiled=True,
    )
    partner = partner.reshape(n_grp, n_dev, bands, bands)
    sym = 0.5 * (rounded.astype(jnp.float32) + jnp.swapaxes(partner, 2, 3).astype(jnp.float32))
    return sym.transpose(1, 2, 0, 3)[:, :, :, None, :]


def solution(mesh):
    return jax.shard_map(
        per_device,
        mesh=mesh,
        in_specs=(
            P(("grp", "dev"), None, None, None),
            P(("grp", "dev"), None, None),
            P(("grp", "dev"), None),
            P(("grp", "dev")),
            P(("grp", "dev")),
        ),
        out_specs=P("grp", None, None, "dev", None),
        check_vma=False,
    )
```

profile of v0, /device:TPU:11, one launch (start us, length us, event | category | flops | bytes accessed | tf_op | source)
XLA Modules:
  0.0 282.3 jit_solution(13385054663650171991)
XLA Ops:
  0.7 0.7 fusion.18
  1.3 0.9 select_reduce_fusion
  2.3 0.7 fusion.21
  2.9 1.0 scatter_custom_fusion
  3.9 0.8 all_to_all.12
  4.7 10.7 %all-to-all-start = ((s32[128,1,2]{2,1,0:T(1,128)}), s32[128,1,2]{2,1,0:T(1,128)S(1)}, u32[]{:S(2)}, u32[]{:S(2)}) async-start(s32[128,1,2]{2,1,0:T(1,128)} %bitcast.4), calls=%async_computation | async-start | bytes 131072 | tf_op jit(solution)/shard_map/all_to_all | solution.py:42
  15.4 0.0 copy-start
  15.4 1.1 add_divide_fusion
  16.6 1.1 slice_bitcast_fusion.2
  17.8 4.1 %slice.29 = bf16[128,1,120,120]{0,3,2,1:T(8,128)(2,1)} slice(bf16[128,2,120,120]{0,3,2,1:T(8,128)(2,1)} %param.5), slice={[0:128], [1:2], [0:120], [0:120]} | slice | bytes 7372800 | tf_op jit(solution)/shard_map/slice | solution.py:19
  21.9 0.0 copy-done
  21.9 2.6 fusion.7
  24.4 6.4 %copy.40 = bf16[128,120,120]{2,1,0:T(8,128)(2,1)} copy(bf16[128,120,120]{0,2,1:T(8,128)(2,1)} %fusion.7) | data formatting | bytes 7372800 | tf_op jit(solution)/shard_map/convert_element_type | solution.py:18
  30.8 0.1 copy.36
  30.9 0.1 copy.35
  31.0 0.1 copy.37
  31.1 0.1 copy.38
  31.2 6.3 %copy.45 = bf16[128,1,120,120]{3,2,0,1:T(8,128)(2,1)} copy(bf16[128,1,120,120]{0,3,2,1:T(8,128)(2,1)} %slice.29) | data formatting | bytes 7372800
  37.5 7.9 %fusion.4 = bf16[128,120,120]{2,1,0:T(8,128)(2,1)} fusion(f32[128,120]{1,0:T(8,128)S(1)} %copy.38, f32[128,120]{1,0:T(8,128)S(1)} %copy.37, f32[128,120]{1,0:T(8,128)S(1)} %copy.36, f32[128,120]{1,0:T(8,128)S(1)} %copy.35, bf16[128,120,120]{2,1,0:T(8,128)(2,1)} %copy.40, bf16[128,1,120,120]{3,2,0,1:T(8,128)(2,1)} %copy.45), kind=kOutput, calls=%fused_computation.8 | convolution fusion | flops 457113600 | bytes 11304960 | tf_op jit(solution)/shard_map/tjk,tlk->tjl/dot_general | solution.py:19
  45.3 4.2 %broadcast_in_dim.28 = bf16[256,120,120]{2,1,0:T(8,128)(2,1)} broadcast(bf16[]{:T(256)} %constant.48.clone.1), dimensions={} | broadcast | bytes 7372802 | tf_op jit(solution)/shard_map/broadcast_in_dim | solution.py:31
  49.5 19.0 %scatter_fusion = bf16[256,120,120]{2,1,0:T(8,128)(2,1)} fusion(bf16[256,120,120]{2,1,0:T(8,128)(2,1)} %broadcast_in_dim.28, s32[128]{0:T(128)S(1)} %fusion.21, bf16[128,120,120]{2,1,0:T(8,128)(2,1)} %fusion.4), kind=kCustom, calls=%fused_computation.1 | custom fusion | bytes 11059712 | tf_op jit(solution)/shard_map/scatter | solution.py:31
  68.5 0.0 all-to-all-done
  68.5 10.3 %all-to-all-start.1 = ((bf16[128,2,120,120]{3,2,1,0:T(8,128)(2,1)}), bf16[128,2,120,120]{3,2,1,0:T(8,128)(2,1)}, u32[]{:S(2)}, u32[]{:S(2)}) async-start(bf16[128,2,120,120]{3,2,1,0:T(8,128)(2,1)} %bitcast.51), calls=%async_computation.1 | async-start | bytes 15728640 | tf_op jit(solution)/shard_map/all_to_all | solution.py:35
  78.9 0.6 broadcast.68
  79.4 0.8 reduce.3
  80.2 0.1 eq.36
  80.3 92.5 %all-to-all-done.1 = bf16[128,2,120,120]{3,2,1,0:T(8,128)(2,1)} async-done(((bf16[128,2,120,120]{3,2,1,0:T(8,128)(2,1)}), bf16[128,2,120,120]{3,2,1,0:T(8,128)(2,1)}, u32[]{:S(2)}, u32[]{:S(2)}) %all-to-all-start.1) | async-done | bytes 7372832 | tf_op jit(solution)/shard_map/all_to_all | solution.py:35
  172.8 12.3 %reshape.47 = bf16[256,14400]{1,0:T(8,128)(2,1)} reshape(bf16[128,2,120,120]{3,2,1,0:T(8,128)(2,1)} %all-to-all-done.1) | data formatting | bytes 14745600 | tf_op jit(solution)/shard_map/reshape | solution.py:46
  185.1 8.1 %convolution_convert_fusion = bf16[128,14400]{0,1:T(8,128)(2,1)} fusion(bf16[256,14400]{1,0:T(8,128)(2,1)} %reshape.47, s32[256]{0:T(256)S(1)} %eq.36), kind=kOutput, calls=%fused_computation.2 | convolution fusion | flops 945594368 | bytes 11060224 | tf_op jit(solution)/shard_map/dot_general | solution.py:51
  193.2 6.3 %copy.42 = bf16[128,120,120]{2,1,0:T(8,128)(2,1)} copy(bf16[128,120,120]{0,2,1:T(8,128)(2,1)} %bitcast.52) | data formatting | bytes 7372800 | tf_op jit(solution)/shard_map/reshape;reshape | solution.py:54
  199.5 12.5 %all-to-all-start.2 = ((bf16[128,120,120]{2,1,0:T(8,128)(2,1)}), bf16[128,120,120]{2,1,0:T(8,128)(2,1)}, u32[]{:S(2)}, u32[]{:S(2)}) async-start(bf16[128,120,120]{2,1,0:T(8,128)(2,1)} %copy.42), calls=%async_computation.2 | async-start | bytes 7864320 | tf_op jit(solution)/shard_map/all_to_all | solution.py:53
  212.0 6.4 %copy.41 = f32[128,14400]{1,0:T(8,128)} copy(bf16[128,14400]{0,1:T(8,128)(2,1)} %convolution_convert_fusion) | data formatting | bytes 11059200 | tf_op jit(solution)/shard_map/convert_element_type | solution.py:61
  218.4 9.2 %reshape.49 = f32[4,32,120,120]{3,2,1,0:T(8,128)} reshape(f32[128,14400]{1,0:T(8,128)} %copy.41) | data formatting | bytes 14745600 | tf_op jit(solution)/shard_map/convert_element_type | solution.py:61
  227.6 32.3 %all-to-all-done.2 = bf16[128,120,120]{2,1,0:T(8,128)(2,1)} async-done(((bf16[128,120,120]{2,1,0:T(8,128)(2,1)}), bf16[128,120,120]{2,1,0:T(8,128)(2,1)}, u32[]{:S(2)}, u32[]{:S(2)}) %all-to-all-start.2) | async-done | bytes 3686432 | tf_op jit(solution)/shard_map/all_to_all | solution.py:53
  260.0 6.9 %copy.43 = f32[4,32,120,120]{2,3,1,0:T(8,128)} copy(bf16[4,32,120,120]{3,2,1,0:T(8,128)(2,1)} %bitcast.19) | data formatting | bytes 11059200 | tf_op jit(solution)/shard_map/convert_element_type | solution.py:61
  266.8 6.2 %fusion.6 = f32[32,120,4,1,120]{4,1,0,2,3:T(8,128)S(1)} fusion(f32[4,32,120,120]{3,2,1,0:T(8,128)} %reshape.49, f32[4,32,120,120]{2,3,1,0:T(8,128)} %copy.43), kind=kLoop, calls=%fused_computation.11 | loop fusion | flops 3686400 | bytes 22118400 | tf_op jit(solution)/shard_map/broadcast_in_dim | solution.py:62
  273.1 9.3 %copy.44 = f32[32,120,4,1,120]{4,3,2,1,0:T(1,128)} copy(f32[32,120,4,1,120]{4,1,0,2,3:T(8,128)S(1)} %fusion.6) | data formatting | bytes 14745600 | tf_op jit(solution)/shard_map/broadcast_in_dim | solution.py:62
  (4 shorter events, 0.1 us)
Async XLA Ops:
  4.7 63.9 %all-to-all-start = ((s32[128,1,2]{2,1,0:T(1,128)}), s32[128,1,2]{2,1,0:T(1,128)S(1)}, u32[]{:S(2)}, u32[]{:S(2)}) async-start(s32[128,1,2]{2,1,0:T(1,128)} %bitcast.4), calls=%async_computation | async-start | bytes 131072 | tf_op jit(solution)/shard_map/all_to_all | solution.py:42
  15.4 6.4 %copy-start = (bf16[128,2,120,120]{0,3,2,1:T(8,128)(2,1)S(1)}, bf16[128,2,120,120]{0,3,2,1:T(8,128)(2,1)}, u32[]{:S(2)}) copy-start(bf16[128,2,120,120]{0,3,2,1:T(8,128)(2,1)} %param.5) | copy-start | bytes 22118404
  68.5 104.3 %all-to-all-start.1 = ((bf16[128,2,120,120]{3,2,1,0:T(8,128)(2,1)}), bf16[128,2,120,120]{3,2,1,0:T(8,128)(2,1)}, u32[]{:S(2)}, u32[]{:S(2)}) async-start(bf16[128,2,120,120]{3,2,1,0:T(8,128)(2,1)} %bitcast.51), calls=%async_computation.1 | async-start | bytes 15728640 | tf_op jit(solution)/shard_map/all_to_all | solution.py:35
  199.5 60.5 %all-to-all-start.2 = ((bf16[128,120,120]{2,1,0:T(8,128)(2,1)}), bf16[128,120,120]{2,1,0:T(8,128)(2,1)}, u32[]{:S(2)}, u32[]{:S(2)}) async-start(bf16[128,120,120]{2,1,0:T(8,128)(2,1)} %copy.42), calls=%async_computation.2 | async-start | bytes 7864320 | tf_op jit(solution)/shard_map/all_to_all | solution.py:53
where the time goes:
time: 287 us; the launch traced here: 282 us
  waiting for transfers between devices  125 us (44%)
  local copies, waits for them, and re-layouts  94.3 us (33%)
  starting transfers between devices  33.5 us (12%)
  matrix products  15.9 us (6%)
  other arithmetic  13 us (5%)
    all_to_all x1, waiting for transfers between devices, per_device(): lax.all_to_all(outgoing.reshape(devices, cap, bands, bands), ('grp', 'dev...  92.5 us
    all_to_all x1, waiting for transfers between devices, per_device(): lax.all_to_all(rounded.reshape(devices, bands, bands), ('grp', 'dev'), sp...  32.3 us
    scatter x1, local copies, waits for them, and re-layouts, per_device(): jnp.zeros((devices * cap, bands, bands), jnp.bfloat16).at[place]  19 us
    convert_element_type x2, local copies, waits for them, and re-layouts, per_device(): rounded.astype(jnp.float32)  15.6 us
    all_to_all x1, starting transfers between devices, per_device(): lax.all_to_all(rounded.reshape(devices, bands, bands), ('grp', 'dev'), sp...  12.5 us
    reshape x1, local copies, waits for them, and re-layouts, per_device(): flat_blocks = got_blocks.reshape(devices * cap, bands * bands)  12.3 us
    all_to_all x1, starting transfers between devices, per_device(): lax.all_to_all(labels.reshape(devices, cap), ('grp', 'dev'), split_axis=0...  10.7 us
    all_to_all x1, starting transfers between devices, per_device(): lax.all_to_all(outgoing.reshape(devices, cap, bands, bands), ('grp', 'dev...  10.3 us
  transfers between devices with their start and end apart: 3, of which 2 were waited for; matrix products, arithmetic and copies ran while one was open for 25% of the time, Pallas kernels for 0%

commit v1 on v0

v1 whole, which is shorter than its diff:
```python
import functools

import jax
import jax.numpy as jnp
import numpy as np
from jax import lax
from jax.experimental import pallas as pl
from jax.experimental.pallas import tpu as pltpu
from jax.sharding import PartitionSpec as P

MESH = pl.DeviceIdType.MESH
LANES = 128
VMEM_BYTES = 56 * 2**20


def offsets_in_balanced_order():
    every = [
        (a, b, c, k) for a in range(4) for b in range(4) for c in range(4) for k in range(2)
    ][1:]
    seen, groups = set(), []
    for first in every:
        if first in seen:
            continue
        group, o = [], first
        for _ in range(3):
            for q in (o, tuple((4 - v) % 4 for v in o[:3]) + (o[3],)):
                if q not in group:
                    group.append(q)
            o = (o[1], o[2], o[0], o[3])
        seen.update(group)
        groups.append(group)
    order = np.random.RandomState(0).permutation(len(groups))
    return [o for g in order for o in groups[g]]


def position():
    g, d = lax.axis_index("grp"), lax.axis_index("dev")
    return g, d // 8, lax.rem(d // 2, 4), lax.rem(d, 2)


def at_offset(pos, off):
    x, y, z, core = pos
    dest_g = lax.rem(x + off[0], 4)
    dest_d = (lax.rem(y + off[1], 4) * 4 + lax.rem(z + off[2], 4)) * 2 + lax.rem(core + off[3], 2)
    return dest_g, dest_d


def enter(pos, offsets):
    barrier = pltpu.get_barrier_semaphore()
    for off in offsets:
        pl.semaphore_signal(
            barrier, inc=1, device_id=at_offset(pos, off), device_id_type=MESH
        )
    pl.semaphore_wait(barrier, len(offsets))


def exchange_kernel(offsets, width, by_tile, src, dst, send_sem, recv_sem, own_sem):
    pos = position()
    g, d = lax.axis_index("grp"), lax.axis_index("dev")
    n_dev = lax.axis_size("dev")
    n_grp = lax.axis_size("grp")
    me = d * n_grp + g if by_tile else g * n_dev + d
    enter(pos, offsets)
    own = pltpu.make_async_copy(
        src.at[pl.ds(me * width, width)], dst.at[pl.ds(me * width, width)], own_sem
    )
    own.start()
    for off in offsets:
        dest_g, dest_d = at_offset(pos, off)
        other = dest_d * n_grp + dest_g if by_tile else dest_g * n_dev + dest_d
        pltpu.make_async_remote_copy(
            src_ref=src.at[pl.ds(other * width, width)],
            dst_ref=dst.at[pl.ds(me * width, width)],
            send_sem=send_sem,
            recv_sem=recv_sem,
            device_id=(dest_g, dest_d),
            device_id_type=MESH,
        ).start()
    rest = pl.ds(0, len(offsets) * width)
    pltpu.make_async_copy(src.at[rest], src.at[rest], send_sem).wait()
    pltpu.make_async_copy(dst.at[rest], dst.at[rest], recv_sem).wait()
    own.wait()


def exchange(blocks, width, by_tile, collective_id, name):
    offsets = offsets_in_balanced_order()
    return pl.pallas_call(
        functools.partial(exchange_kernel, offsets, width, by_tile),
        name=name,
        out_shape=jax.ShapeDtypeStruct(blocks.shape, blocks.dtype),
        in_specs=[pl.BlockSpec(memory_space=pl.ANY)],
        out_specs=pl.BlockSpec(memory_space=pl.ANY),
        scratch_shapes=[pltpu.SemaphoreType.DMA] * 3,
        compiler_params=pltpu.CompilerParams(
            collective_id=collective_id, has_side_effects=True, vmem_limit_bytes=VMEM_BYTES
        ),
    )(blocks)


def blocks_kernel(
    cap, chunk, owner, tile, live, strength, freqs, out, s0, s1, rows, counts
):
    step = pl.program_id(0)
    steps = pl.num_programs(0)
    n_factor, _, bands, trip = strength.shape
    slots = out.shape[0] - 1

    eye = (
        lax.broadcasted_iota(jnp.int32, (trip, trip), 0)
        == lax.broadcasted_iota(jnp.int32, (trip, trip), 1)
    ).astype(jnp.bfloat16)

    @pl.when(step == 0)
    def _():
        occ = 1.0 / (jnp.exp(freqs[0]) - 1.0)
        rowf = jnp.sqrt(occ * (occ + 1.0))
        occ = 1.0 / (jnp.exp(freqs[1]) - 1.0)
        colf = jnp.sqrt(occ * (occ + 1.0))
        for q, value in enumerate((freqs[0], rowf, freqs[1], colf)):
            rows[pl.ds(q, trip, stride=8), 0:bands] = value.T

    third = 1.0 / (jnp.exp(freqs[2]) - 1.0) + 1.0
    for r in range(chunk):
        scaled = (strength[0, r].astype(jnp.float32) * third).astype(jnp.bfloat16)
        for value, store in ((scaled, s0), (strength[1, r], s1)):
            turned = lax.dot_general(
                eye, value, (((1,), (1,)), ((), ())), preferred_element_type=jnp.float32
            )
            store[pl.ds(step * chunk + r, trip, stride=bands), 0:bands] = turned

    @pl.when(step == steps - 1)
    def _():
        dead = jnp.full((16, LANES), -1.0, jnp.bfloat16)

        @pl.loop(0, slots)
        def _(s):
            out[s, 0:16, :] = dead

        @pl.loop(0, counts.shape[0])
        def _(s):
            counts[s] = 0

        lane = lax.broadcasted_iota(jnp.int32, (bands, LANES), 1)

        @pl.loop(0, trip, unroll=4)
        def _(t):
            target = owner[t]
            alive = t < live[0]
            before = counts[target]
            counts[target] = before + alive.astype(jnp.int32)
            place = jnp.where(alive, target * cap + before, slots)
            a = s0[pl.ds(t * bands, bands), 0:bands].astype(jnp.bfloat16)
            b = s1[pl.ds(t * bands, bands), 0:bands].astype(jnp.bfloat16)
            core = lax.dot_general(
                a, b, (((1,), (1,)), ((), ())), preferred_element_type=jnp.float32
            )
            line = rows[pl.ds(pl.multiple_of(t * 8, 8), 8), :]
            column = line.T[0:bands]
            diff = column[:, 0:1] - line[2:3, 0:bands]
            scale = column[:, 1:2] * line[3:4, 0:bands] * jnp.exp(-diff * diff / 0.5)
            value = (scale * core).astype(jnp.bfloat16)
            value = jnp.concatenate(
                [value, jnp.zeros((bands, LANES - bands), jnp.bfloat16)], axis=1
            )
            label = tile[t].astype(jnp.float32).astype(jnp.bfloat16)
            out[place] = jnp.where(lane < bands, value, label)


def make_blocks(strength, freqs, owner, tile, live, cap, devices):
    trip, n_factor, bands, _ = strength.shape
    by_lane = strength.transpose(1, 2, 3, 0)
    freqs = freqs.transpose(1, 2, 0)
    chunk = 4
    smem = pl.BlockSpec(memory_space=pltpu.SMEM)
    return pl.pallas_call(
        functools.partial(blocks_kernel, cap, chunk),
        name="blocks",
        grid=(bands // chunk,),
        out_shape=jax.ShapeDtypeStruct((devices * cap + 1, bands, LANES), jnp.bfloat16),
        in_specs=[
            smem,
            smem,
            smem,
            pl.BlockSpec((n_factor, chunk, bands, trip), lambda i: (0, i, 0, 0)),
            pl.BlockSpec(memory_space=pltpu.VMEM),
        ],
        out_specs=pl.BlockSpec(memory_space=pltpu.VMEM),
        scratch_shapes=[
            pltpu.VMEM((trip * bands, LANES), jnp.float32),
            pltpu.VMEM((trip * bands, LANES), jnp.float32),
            pltpu.VMEM((trip * 8, LANES), jnp.float32),
            pltpu.SMEM((devices,), jnp.int32),
        ],
        compiler_params=pltpu.CompilerParams(vmem_limit_bytes=VMEM_BYTES),
    )(owner, tile, live, by_lane, freqs)


def sum_kernel(labels, got, out, total):
    step = pl.program_id(0)
    here = got.shape[0]

    @pl.when(step == 0)
    def _():
        @pl.loop(0, total.shape[0], unroll=4)
        def _(k):
            total[k] = jnp.zeros(total.shape[1:], jnp.float32)

    @pl.loop(0, here)
    def _(s):
        label = labels[step * here + s]

        @pl.when(label >= 0)
        def _():
            total[label] += got[s].astype(jnp.float32)

    @pl.when(step == pl.num_programs(0) - 1)
    def _():
        @pl.loop(0, total.shape[0], unroll=4)
        def _(k):
            out[k] = total[k].astype(out.dtype)


def sum_tiles(labels, got, tiles):
    slots, bands, lanes = got.shape
    here = 16
    return pl.pallas_call(
        sum_kernel,
        name="sum_tiles",
        grid=(slots // here,),
        out_shape=jax.ShapeDtypeStruct((tiles, bands, lanes), jnp.bfloat16),
        in_specs=[
            pl.BlockSpec(memory_space=pltpu.SMEM),
            pl.BlockSpec((here, bands, lanes), lambda i: (i, 0, 0)),
        ],
        out_specs=pl.BlockSpec(memory_space=pltpu.VMEM),
        scratch_shapes=[pltpu.VMEM((tiles, bands, lanes), jnp.float32)],
        compiler_params=pltpu.CompilerParams(vmem_limit_bytes=VMEM_BYTES),
    )(labels, got)


def symmetrize_kernel(n_grp, omega, partner, out):
    per, bands, lanes = omega.shape
    eye = (
        lax.broadcasted_iota(jnp.int32, (lanes, lanes), 0)
        == lax.broadcasted_iota(jnp.int32, (lanes, lanes), 1)
    ).astype(jnp.bfloat16)
    for k in range(per):
        turned = lax.dot_general(
            eye, partner[k], (((1,), (1,)), ((), ())), preferred_element_type=jnp.float32
        )
        value = 0.5 * (omega[k][:, 0:bands].astype(jnp.float32) + turned[0:bands])
        i, c = divmod(k, n_grp)
        out[i, pl.ds(c, bands, stride=n_grp), :] = value


def symmetrize(omega, partner, n_grp):
    tiles, bands, lanes = omega.shape
    rows = 2
    spec = pl.BlockSpec((rows * n_grp, bands, lanes), lambda i: (i, 0, 0))
    return pl.pallas_call(
        functools.partial(symmetrize_kernel, n_grp),
        name="symmetrize",
        grid=(tiles // (rows * n_grp),),
        out_shape=jax.ShapeDtypeStruct((tiles // n_grp, bands * n_grp, bands), jnp.float32),
        in_specs=[spec, spec],
        out_specs=pl.BlockSpec((rows, bands * n_grp, bands), lambda i: (i, 0, 0)),
        compiler_params=pltpu.CompilerParams(vmem_limit_bytes=VMEM_BYTES),
    )(omega, partner)


def per_device(strength, freqs, owner, tile_slot, live_count):
    trip, _, bands, _ = strength.shape
    n_grp = lax.axis_size("grp")
    n_dev = lax.axis_size("dev")
    devices = n_grp * n_dev
    cap = 2
    outgoing = make_blocks(
        strength, freqs, owner[:, 0], tile_slot, live_count, cap, devices
    )
    got = exchange(outgoing, cap, False, 1, "send_blocks")
    labels = got[:, 0, bands].astype(jnp.int32)
    omega = sum_tiles(labels, got, devices)
    partner = exchange(omega, 1, True, 2, "send_tiles")
    sym = symmetrize(omega, partner, n_grp)
    return sym.reshape(devices // n_grp, bands, n_grp, 1, bands)


def solution(mesh):
    return jax.shard_map(
        per_device,
        mesh=mesh,
        in_specs=(
            P(("grp", "dev"), None, None, None),
            P(("grp", "dev"), None, None),
            P(("grp", "dev"), None),
            P(("grp", "dev")),
            P(("grp", "dev")),
        ),
        out_specs=P("grp", None, None, "dev", None),
        check_vma=False,
    )
```

time: 287 us -> 244 us (0.85)
  Pallas kernels: 0 us -> 232 us
  waiting for transfers between devices: 125 us -> 0 us
  local copies, waits for them, and re-layouts: 94.3 us -> 0 us
  starting transfers between devices: 33.5 us -> 0 us
  matrix products: 15.9 us -> 0 us
  other arithmetic: 13 us -> 6.56 us
    pallas_call x0 -> x5, Pallas kernels: none -> 232 us  [the longest x2 167 us: exchange(): pl.pallas_call(functools.partial(exchange_kernel, offsets, width, by_tile...]
    all_to_all x3 -> x0, waiting for transfers between devices: 125 us -> none  [the longest x1 92.5 us: per_device(): lax.all_to_all(outgoing.reshape(devices, cap, bands, bands), ('grp', 'dev...]
    all_to_all x3 -> x0, starting transfers between devices: 33.5 us -> none  [the longest x1 12.5 us: per_device(): lax.all_to_all(rounded.reshape(devices, bands, bands), ('grp', 'dev'), sp...]
    convert_element_type x4 -> x0, local copies, waits for them, and re-layouts: 28.8 us -> none  [the longest x2 15.6 us: per_device(): rounded.astype(jnp.float32)]
    scatter x2 -> x0, local copies, waits for them, and re-layouts: 20 us -> none  [the longest x1 19 us: per_device(): jnp.zeros((devices * cap, bands, bands), jnp.bfloat16).at[place]]
    dot_general x2 -> x0, matrix products: 15.9 us -> none  [the longest x1 8.05 us: per_device(): omega = jnp.dot(selector, flat_blocks, preferred_element_type=jnp.float32)]
    broadcast_in_dim x2 -> x0, local copies, waits for them, and re-layouts: 13.5 us -> none  [the longest x1 9.28 us: per_device(): return sym.transpose(1, 2, 0, 3)[:, :, :, None, :]]
    reshape x1 -> x0, local copies, waits for them, and re-layouts: 12.3 us -> none  [per_device(): flat_blocks = got_blocks.reshape(devices * cap, bands * bands)]
  transfers between devices with their start and end apart: 3 -> 0, of which waited for: 2 -> 0; matrix products, arithmetic and copies ran while one was open for 25% -> 0% of each run, Pallas kernels for 0% -> 0%
where the time goes in v1:
time: 244 us; the launch traced here: 239 us
  Pallas kernels  232 us (95%)
  other arithmetic  6.56 us (3%)
    pallas_call x2, Pallas kernels, exchange(): pl.pallas_call(functools.partial(exchange_kernel, offsets, width, by_tile...  167 us
    pallas_call x1, Pallas kernels, make_blocks(): pl.pallas_call(functools.partial(blocks_kernel, cap, chunk), name='blocks...  36.5 us
    pallas_call x1, Pallas kernels, sum_tiles(): pl.pallas_call(sum_kernel, name='sum_tiles', grid=(slots // here,), out_s...  14.3 us
    pallas_call x1, Pallas kernels, symmetrize(): pl.pallas_call(functools.partial(symmetrize_kernel, n_grp), name='symmetr...  14 us
    convert_element_type x1, other arithmetic, per_device(): labels = got[:, 0, bands].astype(jnp.int32)  6.56 us

profile of v1, /device:TPU:11, one launch (start us, length us, event | category | flops | bytes accessed | tf_op | source)
XLA Modules:
  0.0 239.2 jit_solution(2360144761202842792)
XLA Ops:
  0.7 36.5 %blocks.1.src = bf16[257,120,128]{2,1,0:T(8,128)(2,1)} custom-call(s32[128]{0:T(128)} %bitcast.8, s32[128]{0:T(128)} %tile.1, s32[1]{0:T(128)S(6)} %copy.8.live, bf16[2,120,120,128]{3,2,1,0:T(8,128)(2,1)} %bitcast.6, f32[3,120,128]{2,1,0:T(8,128)} %bitcast.7), custom_call_target="tpu_custom_call" | custom-call | tf_op jit(solution)/shard_map/blocks/pallas_call | solution.py:175
  37.2 107.0 %send_blocks.1.got = bf16[257,120,128]{2,1,0:T(8,128)(2,1)} custom-call(bf16[257,120,128]{2,1,0:T(8,128)(2,1)} %blocks.1.src), custom_call_target="tpu_custom_call" | custom-call | tf_op jit(solution)/shard_map/send_blocks/pallas_call | solution.py:87
  144.2 6.6 %convert_reduce_fusion.labels = s32[257]{0:T(512)} fusion(bf16[257,120,128]{2,1,0:T(8,128)(2,1)} %send_blocks.1.got), kind=kLoop, calls=%fused_computation | loop fusion | flops 257 | bytes 1542 | tf_op jit(solution)/shard_map/convert_element_type | solution.py:281
  150.8 14.3 %sum_tiles.1.src.omega = bf16[128,120,128]{2,1,0:T(8,128)(2,1)} custom-call(s32[257]{0:T(512)} %convert_reduce_fusion.labels, bf16[257,120,128]{2,1,0:T(8,128)(2,1)} %send_blocks.1.got), custom_call_target="tpu_custom_call" | custom-call | tf_op jit(solution)/shard_map/sum_tiles/pallas_call | solution.py:226
  165.1 60.1 %send_tiles.1.partner = bf16[128,120,128]{2,1,0:T(8,128)(2,1)} custom-call(bf16[128,120,128]{2,1,0:T(8,128)(2,1)} %sum_tiles.1.src.omega), custom_call_target="tpu_custom_call" | custom-call | tf_op jit(solution)/shard_map/send_tiles/pallas_call | solution.py:87
  225.2 14.0 %symmetrize.1 = f32[32,480,120]{2,1,0:T(8,128)} custom-call(bf16[128,120,128]{2,1,0:T(8,128)(2,1)} %sum_tiles.1.src.omega, bf16[128,120,128]{2,1,0:T(8,128)(2,1)} %send_tiles.1.partner), custom_call_target="tpu_custom_call" | custom-call | tf_op jit(solution)/shard_map/symmetrize/pallas_call | solution.py:260

commit v2 on v1

v2 whole, which is shorter than its diff:
```python
import functools

import jax
import jax.numpy as jnp
from jax import lax
from jax.experimental import pallas as pl
from jax.experimental.pallas import tpu as pltpu
from jax.sharding import PartitionSpec as P

MESH = pl.DeviceIdType.MESH
LANES = 128
SIDE = 4
VMEM_BYTES = 56 * 2**20


def position():
    g, d = lax.axis_index("grp"), lax.axis_index("dev")
    return g, d // 8, lax.rem(d // 2, 4), lax.rem(d, 2)


def device_at(pos, axis, step, flip):
    at = list(pos)
    if step:
        at[axis] = lax.rem(pos[axis] + step, SIDE)
    if flip:
        at[3] = 1 - pos[3]
    return at[0], (at[1] * SIDE + at[2]) * 2 + at[3]


def exchange_kernel(places, n, *refs):
    srcs, dsts, firsts, seconds = (refs[k * n : (k + 1) * n] for k in range(4))
    send_sem, recv_sem, own_sem = refs[4 * n :]
    pos = position()
    moves = [[(r, False) for r in (1, 3, 2)]] * 2 + [
        [(r, f) for r in (1, 3, 2) for f in (False, True)] + [(0, True)]
    ]

    barrier = pltpu.get_barrier_semaphore()
    greeted = [(a, r, f) for a in range(3) for r in (1, 2, 3) for f in (False, True)]
    greeted.append((0, 0, True))
    for a, r, f in greeted:
        pl.semaphore_signal(
            barrier, inc=1, device_id=device_at(pos, a, r, f), device_id_type=MESH
        )
    pl.semaphore_wait(barrier, len(greeted))

    def view(ref, whole, p, axis, at, core):
        index = [slice(None)] * 4
        index[places[axis]] = at
        if core is not None:
            index[places[3]] = core
        if whole:
            return ref.at[tuple(index) + (p,)]
        return ref.at[(p,) + tuple(index)]

    def ends(k, stage, p, step, flip):
        axis = (p + stage) % 3
        last = stage == 2
        there = lax.rem(pos[axis] + step, SIDE) if step else pos[axis]
        other = (1 - pos[3] if flip else pos[3]) if last else None
        here = pos[3] if last else None
        source = (srcs, firsts, seconds)[stage][k]
        target = (firsts, seconds, dsts)[stage][k]
        return (
            view(source, stage == 0, p, axis, there, other),
            view(target, last, p, axis, pos[axis], here),
        )

    def own(k, stage, p):
        source, target = ends(k, stage, p, 0, False)
        return pltpu.make_async_copy(source, target, own_sem.at[k, stage, p])

    def remote(k, stage, p, m):
        step, flip = moves[stage][m]
        source, target = ends(k, stage, p, step, flip)
        return pltpu.make_async_remote_copy(
            src_ref=source,
            dst_ref=target,
            send_sem=send_sem.at[k, stage, p, m],
            recv_sem=recv_sem.at[k, stage, p, m],
            device_id=device_at(pos, (p + stage) % 3, step, flip),
            device_id_type=MESH,
        )

    for stage in range(3):
        jobs = [
            (k, stage, p) for p in range(3) for k in range(n) if p < firsts[k].shape[0]
        ]
        for m in range(len(moves[stage])):
            for job in jobs:
                remote(*job, m).start()
        for job in jobs:
            own(*job).start()
        for job in jobs:
            own(*job).wait()
            for m in range(len(moves[stage])):
                remote(*job, m).wait()


def exchange(arrays, places, collective_id, name):
    n = len(arrays)
    thirds = [
        pltpu.VMEM((a.shape[4],) + a.shape[:4] + a.shape[5:], a.dtype) for a in arrays
    ]
    anywhere = [pl.BlockSpec(memory_space=pl.ANY)] * n
    return pl.pallas_call(
        functools.partial(exchange_kernel, places, n),
        name=name,
        out_shape=[jax.ShapeDtypeStruct(a.shape, a.dtype) for a in arrays],
        in_specs=anywhere,
        out_specs=anywhere,
        scratch_shapes=thirds
        + thirds
        + [pltpu.SemaphoreType.DMA((n, 3, 3, 7))] * 2
        + [pltpu.SemaphoreType.DMA((n, 3, 3))],
        compiler_params=pltpu.CompilerParams(
            collective_id=collective_id, has_side_effects=True, vmem_limit_bytes=VMEM_BYTES
        ),
    )(*arrays)


def blocks_kernel(
    chunk, owner, tile, live, strength, freqs, out, labels, s0, s1, rows, counts
):
    step = pl.program_id(0)
    steps = pl.num_programs(0)
    n_factor, _, bands, trip = strength.shape
    cap = out.shape[2]

    eye = (
        lax.broadcasted_iota(jnp.int32, (trip, trip), 0)
        == lax.broadcasted_iota(jnp.int32, (trip, trip), 1)
    ).astype(jnp.bfloat16)

    @pl.when(step == 0)
    def _():
        occ = 1.0 / (jnp.exp(freqs[0]) - 1.0)
        rowf = jnp.sqrt(occ * (occ + 1.0))
        occ = 1.0 / (jnp.exp(freqs[1]) - 1.0)
        colf = jnp.sqrt(occ * (occ + 1.0))
        for q, value in enumerate((freqs[0], rowf, freqs[1], colf)):
            rows[pl.ds(q, trip, stride=8), 0:bands] = value.T

    third = 1.0 / (jnp.exp(freqs[2]) - 1.0) + 1.0
    for r in range(chunk):
        scaled = (strength[0, r].astype(jnp.float32) * third).astype(jnp.bfloat16)
        for value, store in ((scaled, s0), (strength[1, r], s1)):
            turned = lax.dot_general(
                eye, value, (((1,), (1,)), ((), ())), preferred_element_type=jnp.float32
            )
            store[pl.ds(step * chunk + r, trip, stride=bands), 0:bands] = turned

    @pl.when(step == steps - 1)
    def _():
        @pl.loop(0, counts.shape[0])
        def _(s):
            counts[s] = 0
            for r in range(cap):
                labels[s, r] = -1

        @pl.loop(0, trip, unroll=4)
        def _(t):
            target = owner[t]
            alive = t < live[0]
            before = counts[target]
            counts[target] = before + alive.astype(jnp.int32)
            a = s0[pl.ds(t * bands, bands), 0:bands].astype(jnp.bfloat16)
            b = s1[pl.ds(t * bands, bands), 0:bands].astype(jnp.bfloat16)
            core = lax.dot_general(
                a, b, (((1,), (1,)), ((), ())), preferred_element_type=jnp.float32
            )
            line = rows[pl.ds(pl.multiple_of(t * 8, 8), 8), :]
            column = line.T[0:bands]
            diff = column[:, 0:1] - line[2:3, 0:bands]
            scale = column[:, 1:2] * line[3:4, 0:bands] * jnp.exp(-diff * diff / 0.5)
            value = jnp.pad(scale * core, ((0, 0), (0, LANES - bands)))
            value = value.reshape(out.shape[1], out.shape[3], LANES).astype(out.dtype)

            @pl.when(alive)
            def _():
                out[target, :, before] = value
                labels[target, before] = tile[t]


def make_blocks(strength, freqs, owner, tile, live, cap, devices):
    trip, n_factor, bands, _ = strength.shape
    by_lane = strength.transpose(1, 2, 3, 0)
    freqs = freqs.transpose(1, 2, 0)
    chunk = 4
    smem = pl.BlockSpec(memory_space=pltpu.SMEM)
    return pl.pallas_call(
        functools.partial(blocks_kernel, chunk),
        name="blocks",
        grid=(bands // chunk,),
        out_shape=[
            jax.ShapeDtypeStruct((devices, 3, cap, bands // 3, LANES), jnp.bfloat16),
            jax.ShapeDtypeStruct((devices, LANES), jnp.int32),
        ],
        in_specs=[
            smem,
            smem,
            smem,
            pl.BlockSpec((n_factor, chunk, bands, trip), lambda i: (0, i, 0, 0)),
            pl.BlockSpec(memory_space=pltpu.VMEM),
        ],
        out_specs=[pl.BlockSpec(memory_space=pltpu.VMEM), smem],
        scratch_shapes=[
            pltpu.VMEM((trip * bands, LANES), jnp.float32),
            pltpu.VMEM((trip * bands, LANES), jnp.float32),
            pltpu.VMEM((trip * 8, LANES), jnp.float32),
            pltpu.SMEM((devices,), jnp.int32),
        ],
        compiler_params=pltpu.CompilerParams(vmem_limit_bytes=VMEM_BYTES),
    )(owner, tile, live, by_lane, freqs)


def sum_kernel(labels, got, out, total):
    step = pl.program_id(0)
    here, _, cap = got.shape[:3]

    @pl.when(step == 0)
    def _():
        @pl.loop(0, total.shape[0], unroll=4)
        def _(k):
            total[k] = jnp.zeros(total.shape[1:], jnp.float32)

    @pl.loop(0, here)
    def _(s):
        for r in range(cap):
            label = labels[step * here + s, r]

            @pl.when(label >= 0)
            def _():
                total[label] += got[s, :, r].astype(jnp.float32)

    @pl.when(step == pl.num_programs(0) - 1)
    def _():
        @pl.loop(0, total.shape[0], unroll=4)
        def _(k):
            out[k] = total[k].astype(out.dtype)


def sum_tiles(labels, got, tiles):
    devices, thirds, cap, part, lanes = got.shape
    here = 16
    return pl.pallas_call(
        sum_kernel,
        name="sum_tiles",
        grid=(devices // here,),
        out_shape=jax.ShapeDtypeStruct((tiles, thirds, part, lanes), jnp.bfloat16),
        in_specs=[
            pl.BlockSpec(memory_space=pltpu.SMEM),
            pl.BlockSpec((here, thirds, cap, part, lanes), lambda i: (i, 0, 0, 0, 0)),
        ],
        out_specs=pl.BlockSpec(memory_space=pltpu.VMEM),
        scratch_shapes=[pltpu.VMEM((tiles, thirds, part, lanes), jnp.float32)],
        compiler_params=pltpu.CompilerParams(vmem_limit_bytes=VMEM_BYTES),
    )(labels, got)


def symmetrize_kernel(n_grp, omega, partner, out):
    per, thirds, part, lanes = omega.shape
    bands = thirds * part
    eye = (
        lax.broadcasted_iota(jnp.int32, (lanes, lanes), 0)
        == lax.broadcasted_iota(jnp.int32, (lanes, lanes), 1)
    ).astype(jnp.bfloat16)
    for k in range(per):
        other = partner[k].astype(jnp.float32).reshape(bands, lanes).astype(jnp.bfloat16)
        turned = lax.dot_general(
            eye, other, (((1,), (1,)), ((), ())), preferred_element_type=jnp.float32
        )
        mine = omega[k].astype(jnp.float32).reshape(bands, lanes)
        i, c = divmod(k, n_grp)
        out[i, pl.ds(c, bands, stride=n_grp), :] = 0.5 * (mine[:, 0:bands] + turned[0:bands])


def symmetrize(omega, partner, n_grp):
    tiles, thirds, part, lanes = omega.shape
    bands = thirds * part
    rows = 2
    spec = pl.BlockSpec((rows * n_grp, thirds, part, lanes), lambda i: (i, 0, 0, 0))
    return pl.pallas_call(
        functools.partial(symmetrize_kernel, n_grp),
        name="symmetrize",
        grid=(tiles // (rows * n_grp),),
        out_shape=jax.ShapeDtypeStruct((tiles // n_grp, bands * n_grp, bands), jnp.float32),
        in_specs=[spec, spec],
        out_specs=pl.BlockSpec((rows, bands * n_grp, bands), lambda i: (i, 0, 0)),
        compiler_params=pltpu.CompilerParams(vmem_limit_bytes=VMEM_BYTES),
    )(omega, partner)


def per_device(strength, freqs, owner, tile_slot, live_count):
    trip, _, bands, _ = strength.shape
    n_grp = lax.axis_size("grp")
    n_dev = lax.axis_size("dev")
    devices = n_grp * n_dev
    cap = 2
    outgoing, labels = make_blocks(
        strength, freqs, owner[:, 0], tile_slot, live_count, cap, devices
    )
    part = (3, cap, bands // 3, LANES)
    by_grp = (n_grp, SIDE, SIDE, 2)
    got, got_labels = exchange(
        [outgoing.reshape(*by_grp, *part), labels.reshape(*by_grp, 1, 1, LANES)],
        (0, 1, 2, 3),
        1,
        "send_blocks",
    )
    omega = sum_tiles(
        got_labels.reshape(devices, LANES), got.reshape(devices, *part), devices
    )
    by_dev = (SIDE, SIDE, 2, n_grp)
    (partner,) = exchange(
        [omega.reshape(*by_dev, *omega.shape[1:])], (3, 0, 1, 2), 2, "send_tiles"
    )
    partner = partner.reshape(omega.shape)
    sym = symmetrize(omega, partner, n_grp)
    return sym.reshape(devices // n_grp, bands, n_grp, 1, bands)


def solution(mesh):
    return jax.shard_map(
        per_device,
        mesh=mesh,
        in_specs=(
            P(("grp", "dev"), None, None, None),
            P(("grp", "dev"), None, None),
            P(("grp", "dev"), None),
            P(("grp", "dev")),
            P(("grp", "dev")),
        ),
        out_specs=P("grp", None, None, "dev", None),
        check_vma=False,
    )
```

time: 244 us -> 236 us (0.967)
  other arithmetic: 6.56 us -> 0 us
    convert_element_type x1 -> x0, other arithmetic: 6.56 us -> none  [per_device(): labels = got[:, 0, bands].astype(jnp.int32)]
where the time goes in v2:
time: 236 us; the launch traced here: 233 us
  Pallas kernels  232 us (98%)
    pallas_call x2, Pallas kernels, exchange(): pl.pallas_call(functools.partial(exchange_kernel, places, n), name=name,...  153 us
    pallas_call x1, Pallas kernels, make_blocks(): pl.pallas_call(functools.partial(blocks_kernel, chunk), name='blocks', gr...  54.8 us
    pallas_call x1, Pallas kernels, symmetrize(): pl.pallas_call(functools.partial(symmetrize_kernel, n_grp), name='symmetr...  14 us
    pallas_call x1, Pallas kernels, sum_tiles(): pl.pallas_call(sum_kernel, name='sum_tiles', grid=(devices // here,), out...  11.2 us

profile of v2, /device:TPU:11, one launch (start us, length us, event | category | flops | bytes accessed | tf_op | source)
XLA Modules:
  0.0 233.2 jit_solution(1228415724557643557)
XLA Ops:
  0.7 54.8 %blocks.1 = (bf16[128,3,2,40,128]{4,3,2,1,0:T(8,128)(2,1)}, s32[128,128]{1,0:T(8,128)}) custom-call(s32[128]{0:T(128)} %bitcast.20, s32[128]{0:T(128)} %tile.1, s32[1]{0:T(128)S(6)} %copy.7.live, bf16[2,120,120,128]{3,2,1,0:T(8,128)(2,1)} %bitcast.16, f32[3,120,128]{2,1,0:T(8,128)} %bitcast.17), custom_call_target="tpu_custom_call" | custom-call | tf_op jit(solution)/shard_map/blocks/pallas_call | solution.py:191
  55.4 100.8 %send_blocks.1 = (bf16[4,4,4,2,3,2,40,128]{7,6,5,4,3,2,1,0:T(8,128)(2,1)}, s32[4,4,4,2,1,1,128]{6,5,4,3,2,1,0:T(1,128)}) custom-call(bf16[4,4,4,2,3,2,40,128]{7,6,5,4,3,2,1,0:T(8,128)(2,1)} %bitcast.14, s32[4,4,4,2,1,1,128]{6,5,4,3,2,1,0:T(1,128)} %bitcast.18), custom_call_target="tpu_custom_call" | custom-call | tf_op jit(solution)/shard_map/send_blocks/pallas_call | solution.py:106
  156.2 11.2 %sum_tiles.1.omega = bf16[128,3,40,128]{3,2,1,0:T(8,128)(2,1)} custom-call(s32[128,128]{1,0:T(8,128)} %bitcast.19, bf16[128,3,2,40,128]{4,3,2,1,0:T(8,128)(2,1)} %bitcast.15), custom_call_target="tpu_custom_call" | custom-call | tf_op jit(solution)/shard_map/sum_tiles/pallas_call | solution.py:246
  167.4 51.7 %send_tiles.1 = bf16[4,4,2,4,3,40,128]{6,5,4,3,2,1,0:T(8,128)(2,1)} custom-call(bf16[4,4,2,4,3,40,128]{6,5,4,3,2,1,0:T(8,128)(2,1)} %bitcast.12), custom_call_target="tpu_custom_call" | custom-call | tf_op jit(solution)/shard_map/send_tiles/pallas_call | solution.py:106
  219.2 14.0 %symmetrize.1 = f32[32,480,120]{2,1,0:T(8,128)} custom-call(bf16[128,3,40,128]{3,2,1,0:T(8,128)(2,1)} %sum_tiles.1.omega, bf16[128,3,40,128]{3,2,1,0:T(8,128)(2,1)} %bitcast.13), custom_call_target="tpu_custom_call" | custom-call | tf_op jit(solution)/shard_map/symmetrize/pallas_call | solution.py:283

commit v3 on v2

v3 whole, which is shorter than its diff:
```python
import functools

import jax
import jax.numpy as jnp
from jax import lax
from jax.experimental import pallas as pl
from jax.experimental.pallas import tpu as pltpu
from jax.sharding import PartitionSpec as P

MESH = pl.DeviceIdType.MESH
LANES = 128
SIDE = 4
VMEM_BYTES = 56 * 2**20


PARTS = 3
WALK = 400


def position():
    g, d = lax.axis_index("grp"), lax.axis_index("dev")
    return g, d // 8, lax.rem(d // 2, 4), lax.rem(d, 2)


def device_at(pos, axis, step, flip):
    at = list(pos)
    if step:
        at[axis] = lax.rem(pos[axis] + step, SIDE)
    if flip:
        at[3] = 1 - pos[3]
    return at[0], (at[1] * SIDE + at[2]) * 2 + at[3]


def exchange_kernel(plans, *refs):
    n = len(plans)
    n_shared = sum(plan[2] for plan in plans)
    srcs, dsts, refs = refs[:n], refs[n : 2 * n], refs[2 * n :]
    shared_dsts, refs = refs[:n_shared], refs[n_shared:]
    firsts, seconds, refs = refs[:n], refs[n : 2 * n], refs[2 * n :]
    shared_in, refs = refs[:n_shared], refs[n_shared:]
    send_sem, recv_sem, own_sem = refs
    pos = position()

    barrier = pltpu.get_barrier_semaphore()
    greeted = [(a, r, f) for a in range(3) for r in (1, 2, 3) for f in (False, True)]
    greeted.append((0, 0, True))
    for a, r, f in greeted:
        pl.semaphore_signal(
            barrier, inc=1, device_id=device_at(pos, a, r, f), device_id_type=MESH
        )
    pl.semaphore_wait(barrier, len(greeted))

    def view(ref, places, front, p, axis, at, core):
        index = [slice(None)] * 4
        index[places[axis]] = at
        if core is not None:
            index[places[3]] = core
        return ref.at[(p,) + tuple(index)] if front else ref.at[tuple(index) + (p,)]

    def ends(k, stage, p, step, flip):
        src_places, dst_places, _ = plans[k]
        axis = (p + stage) % 3
        there = lax.rem(pos[axis] + step, SIDE) if step else pos[axis]
        if stage == 0:
            return (
                view(srcs[k], src_places, False, p, axis, there, None),
                view(firsts[k], src_places, True, p, axis, pos[axis], None),
            )
        if stage == 1:
            return (
                view(firsts[k], src_places, True, p, axis, there, None),
                view(seconds[k], src_places, True, p, axis, pos[axis], None),
            )
        if flip is None:
            index = [slice(None)] * 3
            index[axis] = pos[axis]
            return (
                view(seconds[k], src_places, True, p, axis, there, 2),
                shared_in[0].at[(p,) + tuple(index)],
            )
        core = 1 - pos[3] if flip else pos[3]
        return (
            view(seconds[k], src_places, True, p, axis, there, core),
            view(dsts[k], dst_places, False, p, axis, pos[axis], pos[3]),
        )

    def moves(k, stage):
        steps = (1, 3, 2)
        if stage < 2:
            return [(r, False) for r in steps]
        most = [(r, f) for r in steps for f in (False, True)] + [(0, True)]
        return ([(r, None) for r in steps] if plans[k][2] else []) + most

    def own(k, stage, p, shared=False):
        source, target = ends(k, stage, p, 0, None if shared else False)
        return pltpu.make_async_copy(source, target, own_sem.at[k, stage + shared, p])

    def remote(k, stage, p, m):
        step, flip = moves(k, stage)[m]
        source, target = ends(k, stage, p, step, flip)
        return pltpu.make_async_remote_copy(
            src_ref=source,
            dst_ref=target,
            send_sem=send_sem.at[k, stage, p, m],
            recv_sem=recv_sem.at[k, stage, p, m],
            device_id=device_at(pos, (p + stage) % 3, step, bool(flip)),
            device_id_type=MESH,
        )

    def pass_on(p):
        target = shared_dsts[0].at[:, :, :, pos[3], p]
        there = pltpu.make_async_remote_copy(
            src_ref=shared_in[0].at[p],
            dst_ref=target,
            send_sem=send_sem.at[0, 3, p, 0],
            recv_sem=recv_sem.at[0, 3, p, 0],
            device_id=device_at(pos, 0, 0, True),
            device_id_type=MESH,
        )
        return there, pltpu.make_async_copy(shared_in[0].at[p], target, own_sem.at[0, 4, p])

    def jobs(p):
        return [k for k in range(n) if p < firsts[k].shape[0]]

    def start(stage, p):
        for k in jobs(p):
            for m in range(len(moves(k, stage))):
                remote(k, stage, p, m).start()
            own(k, stage, p).start()
            if stage == 2 and plans[k][2]:
                own(k, stage, p, True).start()

    def arrive(stage, p, which=None):
        for k in jobs(p):
            for m, (_, flip) in enumerate(moves(k, stage)):
                if which is None or which == (flip is None):
                    remote(k, stage, p, m).wait_recv()
            if not which:
                own(k, stage, p).wait()
            if stage == 2 and plans[k][2] and which is not False:
                own(k, stage, p, True).wait()

    for p in range(PARTS):
        start(0, p)
    for stage in (1, 2):
        for p in range(PARTS):
            arrive(stage - 1, p)
            start(stage, p)
    if n_shared:
        for p in range(PARTS):
            arrive(2, p, True)
            for copy in pass_on(p):
                copy.start()
    for p in range(PARTS):
        arrive(2, p, False)
    if n_shared:
        for p in range(PARTS):
            there, here = pass_on(p)
            there.wait()
            here.wait()
    for p in range(PARTS):
        for stage in range(3):
            for k in jobs(p):
                for m in range(len(moves(k, stage))):
                    remote(k, stage, p, m).wait_send()


def exchange(arrays, plans, collective_id, name):
    n = len(arrays)
    outs, shared_outs, temps, shared_temps = [], [], [], []
    for a, (src_places, dst_places, shared) in zip(arrays, plans):
        front = [0] * 4
        for axis in range(4):
            front[dst_places[axis]] = 2 if axis == 3 else SIDE
        rest = a.shape[4:]
        outs.append(jax.ShapeDtypeStruct((*front, *rest), a.dtype))
        temps.append(pltpu.VMEM((rest[0],) + a.shape[:4] + rest[1:], a.dtype))
        if shared:
            shared_outs.append(jax.ShapeDtypeStruct((SIDE, SIDE, SIDE, 2, *rest), a.dtype))
            shared_temps.append(pltpu.VMEM((rest[0], SIDE, SIDE, SIDE) + rest[1:], a.dtype))
    outs = outs + shared_outs
    anywhere = pl.BlockSpec(memory_space=pl.ANY)
    return pl.pallas_call(
        functools.partial(exchange_kernel, plans),
        name=name,
        out_shape=outs,
        in_specs=[anywhere] * n,
        out_specs=[anywhere] * len(outs),
        scratch_shapes=temps
        + temps
        + shared_temps
        + [pltpu.SemaphoreType.DMA((n, 4, PARTS, 10))] * 2
        + [pltpu.SemaphoreType.DMA((n, 5, PARTS))],
        compiler_params=pltpu.CompilerParams(
            collective_id=collective_id, has_side_effects=True, vmem_limit_bytes=VMEM_BYTES
        ),
    )(*arrays)


def plan_dense(grid, owner, tile, n_live, labels, cell, place, flip, left):
    n_grp, n_dev = grid
    chips = n_grp * n_dev // 2

    @pl.loop(0, n_live)
    def _(t):
        o = owner[t]
        e = lax.rem(o, 2) * chips + lax.div(o, 2)
        r = (cell[e] >= 0).astype(jnp.int32)
        cell[e] = t
        place[t] = e + r * 2 * chips
        labels[o, r] = tile[t]


def plan_shared(grid, owner, tile, n_live, labels, cell, place, flip, left):
    n_grp, n_dev = grid
    devices = n_grp * n_dev
    chips = devices // 2

    def first(t, n):
        o = owner[t]
        e = lax.rem(o, 2) * chips + lax.div(o, 2)
        taken = cell[e] >= 0

        @pl.when(jnp.logical_not(taken))
        def _():
            cell[e] = t
            place[t] = e
            labels[o, 0] = tile[t]

        @pl.when(taken)
        def _():
            left[n] = t

        return n + taken.astype(jnp.int32)

    n_left = lax.fori_loop(0, n_live, first, jnp.int32(0))

    def insert(q, carry):
        lost, noise = carry

        def body(state):
            t, steps, noise = state
            o, k = owner[t], tile[t]
            x = lax.rem(k, n_grp) * n_dev + lax.div(k, n_grp)
            e0 = lax.rem(o, 2) * chips + lax.div(o, 2)
            e1 = devices + lax.div(o, 2)
            e2 = lax.rem(x, 2) * chips + lax.div(x, 2)
            e3 = devices + lax.div(x, 2)
            noise = lax.rem(noise * 1103 + 12345, 65521)
            pick = lax.rem(lax.div(noise, 8), 4)
            for r, e in ((3, e3), (2, e2), (0, e0), (1, e1)):
                pick = jnp.where(cell[e] < 0, r, pick)
            e = jnp.where(pick == 0, e0, jnp.where(pick == 1, e1, jnp.where(pick == 2, e2, e3)))
            turned = pick >= 2
            to = jnp.where(turned, x, o)
            label = jnp.where(turned, lax.rem(o, n_dev) * n_grp + lax.div(o, n_dev), k)
            victim = cell[e]
            cell[e] = t
            place[t] = e
            flip[t] = turned.astype(jnp.int32)
            both = (e >= devices).astype(jnp.int32)
            labels[to, both] = label

            @pl.when(e >= devices)
            def _():
                labels[to + 1 - 2 * lax.rem(to, 2), 1] = -1

            return victim, steps + 1, noise

        t, _, noise = lax.while_loop(
            lambda state: (state[0] >= 0) & (state[1] < WALK), body, (left[q], 0, noise)
        )
        return lost | (t >= 0).astype(jnp.int32), noise

    lost, _ = lax.fori_loop(0, n_left, insert, (jnp.int32(0), jnp.int32(1)))

    @pl.when(lost > 0)
    def _():
        @pl.loop(0, devices)
        def _(o):
            labels[o, 2] = 1


def blocks_kernel(
    grid, plan, group, owner, tile, live, strength, freqs, out, labels,
    here, turned, rows, block, cell, place, flip, left, in_sem, out_sem,
):
    _, bands, _, trip = strength.shape
    devices = grid[0] * grid[1]
    pieces = in_sem.shape[0]
    piece = bands // pieces

    def fetch(i):
        part = pl.ds(i * piece, piece)
        return pltpu.make_async_copy(strength.at[:, part], here.at[:, part], in_sem.at[i])

    for i in range(pieces):
        fetch(i).start()

    @pl.loop(0, devices, unroll=8)
    def _(o):
        labels[o, 0] = -1
        labels[o, 1] = -1
        labels[o, 2] = 0

    @pl.loop(0, cell.shape[0], unroll=8)
    def _(e):
        cell[e] = -1

    @pl.loop(0, trip, unroll=8)
    def _(t):
        place[t] = -1
        flip[t] = 0

    plan(grid, owner, tile, live[0], labels, cell, place, flip, left)

    lines = []
    for mode in (0, 1):
        occ = 1.0 / (jnp.exp(freqs[mode]) - 1.0)
        lines.append((freqs[mode].T, jnp.sqrt(occ * (occ + 1.0)).T))
    for f in (0, 1):
        for q, value in enumerate(lines[f] + lines[1 - f]):
            rows[pl.ds(f * trip * 8 + q, trip, stride=8), 0:bands] = value
    third = 1.0 / (jnp.exp(freqs[2]) - 1.0) + 1.0
    eye = (
        lax.broadcasted_iota(jnp.int32, (trip, trip), 0)
        == lax.broadcasted_iota(jnp.int32, (trip, trip), 1)
    ).astype(jnp.bfloat16)

    for i in range(pieces):
        fetch(i).wait()

        @pl.loop(i * piece, (i + 1) * piece, unroll=4)
        def _(j):
            scaled = (here[0, j].astype(jnp.float32) * third).astype(jnp.bfloat16)
            turned[pl.ds(j, trip, stride=bands), 0:bands] = scaled.T.astype(jnp.float32)
            other = lax.dot_general(
                eye, here[1, j], (((1,), (1,)), ((), ())), preferred_element_type=jnp.float32
            )
            turned[pl.ds(trip * bands + j, trip, stride=bands), 0:bands] = other

    def send(t):
        e = place[t]
        return pltpu.make_async_copy(block.at[t], out.at[e], out_sem)

    @pl.loop(0, trip // group)
    def _(g):
        for u in range(group):
            t = g * group + u
            f = flip[t]
            factors = [
                turned[pl.ds(pl.multiple_of((h * trip + t) * bands, 8), bands), 0:bands].astype(
                    jnp.bfloat16
                )
                for h in (f, 1 - f)
            ]
            core = lax.dot_general(
                *factors, (((1,), (1,)), ((), ())), preferred_element_type=jnp.float32
            )
            line = rows[pl.ds(pl.multiple_of((f * trip + t) * 8, 8), 8), :]
            column = line.T[0:bands]
            diff = column[:, 0:1] - line[2:3, 0:bands]
            scale = column[:, 1:2] * line[3:4, 0:bands] * jnp.exp(-diff * diff / 0.5)
            value = jnp.pad(scale * core, ((0, 0), (0, LANES - bands)))
            block[t] = value.reshape(block.shape[1:]).astype(block.dtype)
        for u in range(group):
            t = g * group + u

            @pl.when(place[t] >= 0)
            def _():
                send(t).start()

    @pl.loop(0, trip)
    def _(t):
        @pl.when(place[t] >= 0)
        def _():
            send(t).wait()


def make_blocks(strength, freqs, owner, tile, live, grid, plan, cells):
    trip, n_factor, bands, _ = strength.shape
    devices = grid[0] * grid[1]
    by_lane = strength.transpose(1, 2, 3, 0)
    freqs = freqs.transpose(1, 2, 0)
    smem = pl.BlockSpec(memory_space=pltpu.SMEM)
    anywhere = pl.BlockSpec(memory_space=pl.ANY)
    part = (PARTS, bands // PARTS, LANES)
    pieces = 6
    return pl.pallas_call(
        functools.partial(blocks_kernel, grid, plan, 8),
        name="blocks",
        out_shape=[
            jax.ShapeDtypeStruct((cells, *part), jnp.bfloat16),
            jax.ShapeDtypeStruct((devices, LANES), jnp.int32),
        ],
        in_specs=[smem, smem, smem, anywhere, pl.BlockSpec(memory_space=pltpu.VMEM)],
        out_specs=[anywhere, smem],
        scratch_shapes=[
            pltpu.VMEM(by_lane.shape, by_lane.dtype),
            pltpu.VMEM((2 * trip * bands, LANES), jnp.float32),
            pltpu.VMEM((2 * trip * 8, LANES), jnp.float32),
            pltpu.VMEM((trip, *part), jnp.bfloat16),
            pltpu.SMEM((cells,), jnp.int32),
            pltpu.SMEM((trip,), jnp.int32),
            pltpu.SMEM((trip,), jnp.int32),
            pltpu.SMEM((trip,), jnp.int32),
            pltpu.SemaphoreType.DMA((pieces,)),
            pltpu.SemaphoreType.DMA,
        ],
        compiler_params=pltpu.CompilerParams(vmem_limit_bytes=VMEM_BYTES),
    )(owner, tile, live, by_lane, freqs)


def sum_kernel(labels, one, two, out, total):
    step = pl.program_id(0)
    here = one.shape[0]
    tiles = out.shape[0]

    @pl.when(step == 0)
    def _():
        @pl.loop(0, tiles, unroll=4)
        def _(k):
            total[k] = jnp.zeros(total.shape[1:], jnp.float32)

    @pl.loop(0, here, unroll=4)
    def _(s):
        for r, got in enumerate((one, two)):
            label = labels[step * here + s, r]
            total[jnp.where(label < 0, tiles, label)] += got[s].astype(jnp.float32)

    @pl.when(step == pl.num_programs(0) - 1)
    def _():
        @pl.loop(0, tiles, unroll=4)
        def _(k):
            out[k] = total[k].astype(out.dtype)


def sum_tiles(labels, one, two, tiles):
    devices, *part = one.shape
    here = 32
    spec = pl.BlockSpec((here, *part), lambda i: (i, 0, 0, 0))
    return pl.pallas_call(
        sum_kernel,
        name="sum_tiles",
        grid=(devices // here,),
        out_shape=jax.ShapeDtypeStruct((tiles, *part), jnp.bfloat16),
        in_specs=[pl.BlockSpec(memory_space=pltpu.SMEM), spec, spec],
        out_specs=pl.BlockSpec(memory_space=pltpu.VMEM),
        scratch_shapes=[pltpu.VMEM((tiles + 1, *part), jnp.float32)],
        compiler_params=pltpu.CompilerParams(vmem_limit_bytes=VMEM_BYTES),
    )(labels, one, two)


def symmetrize_kernel(n_grp, omega, partner, out):
    per, thirds, part, lanes = omega.shape
    bands = thirds * part
    for k in range(per):
        turned = partner[k].astype(jnp.float32).reshape(bands, lanes).T
        mine = omega[k].astype(jnp.float32).reshape(bands, lanes)
        i, c = divmod(k, n_grp)
        out[i, pl.ds(c, bands, stride=n_grp), :] = 0.5 * (mine[:, 0:bands] + turned[0:bands])


def symmetrize(omega, partner, n_grp):
    tiles, thirds, part, lanes = omega.shape
    bands = thirds * part
    rows = 8
    spec = pl.BlockSpec((rows * n_grp, thirds, part, lanes), lambda i: (i, 0, 0, 0))
    return pl.pallas_call(
        functools.partial(symmetrize_kernel, n_grp),
        name="symmetrize",
        grid=(tiles // (rows * n_grp),),
        out_shape=jax.ShapeDtypeStruct((tiles // n_grp, bands * n_grp, bands), jnp.float32),
        in_specs=[spec, spec],
        out_specs=pl.BlockSpec((rows, bands * n_grp, bands), lambda i: (i, 0, 0)),
        compiler_params=pltpu.CompilerParams(vmem_limit_bytes=VMEM_BYTES),
    )(omega, partner)


def per_device(strength, freqs, owner, tile_slot, live_count):
    bands = strength.shape[2]
    n_grp = lax.axis_size("grp")
    n_dev = lax.axis_size("dev")
    grid = (n_grp, n_dev)
    devices = n_grp * n_dev
    part = (PARTS, bands // PARTS, LANES)
    torus = (SIDE, SIDE, SIDE)
    plain = ((0, 1, 2, 3), (0, 1, 2, 3), False)
    args = (strength, freqs, owner[:, 0], tile_slot, live_count, grid)

    def with_labels(labels):
        return labels.reshape(*torus, 2, 1, 1, LANES)

    cells, labels = make_blocks(*args, plan_shared, devices * 3 // 2)
    own, labels, shared = exchange(
        [cells.reshape(3, *torus, *part), with_labels(labels)],
        [((1, 2, 3, 0), (0, 1, 2, 3), True), plain],
        1,
        "send_blocks",
    )
    labels = labels.reshape(devices, LANES)

    def sum_shared():
        return sum_tiles(
            labels, own.reshape(devices, *part), shared.reshape(devices, *part), devices
        )

    def sum_dense():
        cells, labels = make_blocks(*args, plan_dense, devices * 2)
        cells = cells.reshape(2, 2, *torus, *part)
        moved = ((1, 2, 3, 0), (0, 1, 2, 3), False)
        one, two, labels = exchange(
            [cells[0], cells[1], with_labels(labels)], [moved, moved, plain], 3, "send_dense"
        )
        return sum_tiles(
            labels.reshape(devices, LANES),
            one.reshape(devices, *part),
            two.reshape(devices, *part),
            devices,
        )

    omega = lax.cond(jnp.any(labels[:, 2] > 0), sum_dense, sum_shared)
    by_dev = ((3, 0, 1, 2), (3, 0, 1, 2), False)
    (partner,) = exchange(
        [omega.reshape(SIDE, SIDE, 2, n_grp, *part)], [by_dev], 2, "send_tiles"
    )
    sym = symmetrize(omega, partner.reshape(omega.shape), n_grp)
    return sym.reshape(devices // n_grp, bands, n_grp, 1, bands)


def solution(mesh):
    return jax.shard_map(
        per_device,
        mesh=mesh,
        in_specs=(
            P(("grp", "dev"), None, None, None),
            P(("grp", "dev"), None, None),
            P(("grp", "dev"), None),
            P(("grp", "dev")),
            P(("grp", "dev")),
        ),
        out_specs=P("grp", None, None, "dev", None),
        check_vma=False,
    )
```

time: 236 us -> 177 us (0.75)
  Pallas kernels: 232 us -> 172 us
    pallas_call x3, Pallas kernels: 207 us -> 158 us  [the longest x2 137 us: exchange(): pl.pallas_call(functools.partial(exchange_kernel, plans), name=name, out_...]
    pallas_call x1, Pallas kernels: 14 us -> 6.13 us  [symmetrize(): pl.pallas_call(functools.partial(symmetrize_kernel, n_grp), name='symmetr...]
    pallas_call x1, Pallas kernels: 11.2 us -> 7.86 us  [sum_tiles(): pl.pallas_call(sum_kernel, name='sum_tiles', grid=(devices // here,), out...]
where the time goes in v3:
time: 177 us; the launch traced here: 174 us
  Pallas kernels  172 us (97%)
    pallas_call x2, Pallas kernels, exchange(): pl.pallas_call(functools.partial(exchange_kernel, plans), name=name, out_...  137 us
    pallas_call x1, Pallas kernels, make_blocks(): pl.pallas_call(functools.partial(blocks_kernel, grid, plan, 8), name='blo...  21.3 us
    pallas_call x1, Pallas kernels, sum_tiles(): pl.pallas_call(sum_kernel, name='sum_tiles', grid=(devices // here,), out...  7.86 us
    pallas_call x1, Pallas kernels, symmetrize(): pl.pallas_call(functools.partial(symmetrize_kernel, n_grp), name='symmetr...  6.13 us

profile of v3, /device:TPU:11, one launch (start us, length us, event | category | flops | bytes accessed | tf_op | source)
XLA Modules:
  0.0 174.2 jit_solution(3891157042610892885)
XLA Ops:
  0.7 21.3 %blocks.3 = (bf16[192,3,40,128]{3,2,1,0:T(8,128)(2,1)}, s32[128,128]{1,0:T(8,128)}) custom-call(s32[128]{0:T(128)} %bitcast.39, s32[128]{0:T(128)} %tile.1, s32[1]{0:T(128)S(6)} %copy.9.live, bf16[2,120,120,128]{3,2,1,0:T(8,128)(2,1)} %bitcast.22, f32[3,120,128]{2,1,0:T(8,128)} %bitcast.32), custom_call_target="tpu_custom_call" | custom-call | tf_op jit(solution)/shard_map/blocks/pallas_call | solution.py:389
  22.0 0.0 copy-start.1
  22.0 0.0 copy-start.2
  22.0 0.0 copy-start.3
  22.0 83.4 %send_blocks.1 = (bf16[4,4,4,2,3,40,128]{6,5,4,3,2,1,0:T(8,128)(2,1)}, s32[4,4,4,2,1,1,128]{6,5,4,3,2,1,0:T(1,128)S(1)}, bf16[4,4,4,2,3,40,128]{6,5,4,3,2,1,0:T(8,128)(2,1)}) custom-call(bf16[3,4,4,4,3,40,128]{6,5,4,3,2,1,0:T(8,128)(2,1)} %bitcast.27, s32[4,4,4,2,1,1,128]{6,5,4,3,2,1,0:T(1,128)} %bitcast.37), custom_call_target="tpu_custom_call" | custom-call | tf_op jit(solution)/shard_map/send_blocks/pallas_call | solution.py:183
  105.5 0.7 fusion
  106.8 0.0 copy-done.1
  106.9 0.0 copy-done.2
  106.9 0.0 copy-done.3
  106.9 7.9 %conditional.1 = (bf16[128,3,40,128]{3,2,1,0:T(8,128)(2,1)}) conditional(s32[]{:T(128)} %convert_element_type.3, (bf16[4,4,4,2,3,40,128]{6,5,4,3,2,1,0:T(8,128)(2,1)}, bf16[4,4,4,2,3,40,128]{6,5,4,3,2,1,0:T(8,128)(2,1)}, s32[128,128]{1,0:T(8,128)S(1)}) %tuple.17, (bf16[128,2,120,120]{0,3,2,1:T(8,128)(2,1)}, f32[128,3,120]{0,2,1:T(8,128)S(1)}, ...), branch_computations={%region_1.0_spmd, %region_2.0_spmd} | conditional | bytes 15728648 | solution.py:522
  106.9 7.9 %sum_tiles.2 = bf16[128,3,40,128]{3,2,1,0:T(8,128)(2,1)} custom-call(s32[128,128]{1,0:T(8,128)S(1)} %get-tuple-element.24.labels, bf16[128,3,40,128]{3,2,1,0:T(8,128)(2,1)} %bitcast.28, bf16[128,3,40,128]{3,2,1,0:T(8,128)(2,1)} %bitcast.29), custom_call_target="tpu_custom_call" | custom-call | tf_op jit(solution)/shard_map/cond/branch_0_fun/sum_tiles/pallas_call | solution.py:442
  114.8 0.0 copy-start
  114.8 53.3 %send_tiles.1 = bf16[4,4,2,4,3,40,128]{6,5,4,3,2,1,0:T(8,128)(2,1)} custom-call(bf16[4,4,2,4,3,40,128]{6,5,4,3,2,1,0:T(8,128)(2,1)} %bitcast.21), custom_call_target="tpu_custom_call" | custom-call | tf_op jit(solution)/shard_map/send_tiles/pallas_call | solution.py:183
  168.0 0.0 copy-done
  168.1 6.1 %symmetrize.1 = f32[32,480,120]{2,1,0:T(8,128)} custom-call(bf16[128,3,40,128]{3,2,1,0:T(8,128)(2,1)S(1)} %copy-done, bf16[128,3,40,128]{3,2,1,0:T(8,128)(2,1)} %bitcast.26), custom_call_target="tpu_custom_call" | custom-call | tf_op jit(solution)/shard_map/symmetrize/pallas_call | solution.py:469
Async XLA Ops:
  22.0 84.8 %copy-start.1 = (f32[128,3,120]{0,2,1:T(8,128)S(1)}, f32[128,3,120]{0,2,1:T(8,128)}, u32[]{:S(2)}) copy-start(f32[128,3,120]{0,2,1:T(8,128)} %param.8) | copy-start | bytes 552964
  22.0 84.8 %copy-start.2 = (s32[128,1]{0,1:T(1,128)S(1)}, s32[128,1]{0,1:T(1,128)}, u32[]{:S(2)}) copy-start(s32[128,1]{0,1:T(1,128)} %param.9) | copy-start | bytes 1540
  22.0 84.8 %copy-start.3 = (s32[128]{0:T(128)S(1)}, s32[128]{0:T(128)}, u32[]{:S(2)}) copy-start(s32[128]{0:T(128)} %tile.1) | copy-start | bytes 1540
  114.8 53.3 %copy-start = (bf16[128,3,40,128]{3,2,1,0:T(8,128)(2,1)S(1)}, bf16[128,3,40,128]{3,2,1,0:T(8,128)(2,1)}, u32[]{:S(2)}) copy-start(bf16[128,3,40,128]{3,2,1,0:T(8,128)(2,1)} %get-tuple-element.49.omega) | copy-start | bytes 11796484

commit v4 on v3

v4 whole, which is shorter than its diff:
```python
import functools

import jax
import jax.numpy as jnp
from jax import lax
from jax.experimental import pallas as pl
from jax.experimental.pallas import tpu as pltpu
from jax.sharding import PartitionSpec as P

MESH = pl.DeviceIdType.MESH
LANES = 128
SIDE = 4
VMEM_BYTES = 56 * 2**20


PARTS = 3
WALK = 400
PIECES = 6


def position():
    g, d = lax.axis_index("grp"), lax.axis_index("dev")
    return g, d // 8, lax.rem(d // 2, 4), lax.rem(d, 2)


def device_at(pos, axis, step, flip):
    at = list(pos)
    if step:
        at[axis] = lax.rem(pos[axis] + step, SIDE)
    if flip:
        at[3] = 1 - pos[3]
    return at[0], (at[1] * SIDE + at[2]) * 2 + at[3]


def exchange_kernel(plans, *refs):
    n = len(plans)
    srcs, dsts, firsts, seconds = (refs[k * n : (k + 1) * n] for k in range(4))
    send_sem, recv_sem, own_sem = refs[4 * n :]
    pos = position()
    steps = (1, 3, 2)

    barrier = pltpu.get_barrier_semaphore()
    greeted = [(a, r, f) for a in range(3) for r in (1, 2, 3) for f in (False, True)]
    greeted.append((0, 0, True))
    for a, r, f in greeted:
        pl.semaphore_signal(
            barrier, inc=1, device_id=device_at(pos, a, r, f), device_id_type=MESH
        )
    pl.semaphore_wait(barrier, len(greeted))

    def view(ref, places, front, p, axis, at, core):
        index = [slice(None)] * 4
        index[places[axis]] = at
        index[places[3]] = core
        return ref.at[(p,) + tuple(index)] if front else ref.at[tuple(index) + (p,)]

    def ends(stage, k, f, p, step):
        src_places, dst_places = plans[k]
        axis = (p + stage) % 3
        there = lax.rem(pos[axis] + step, SIDE) if step else pos[axis]
        core = (pos[3], 1 - pos[3])[f]
        source = view((srcs, firsts, seconds)[stage][k], src_places, stage > 0, p, axis, there, core)
        if stage < 2:
            target = view((firsts, seconds)[stage][k], src_places, True, p, axis, pos[axis], core)
        else:
            target = view(dsts[k], dst_places, False, p, axis, pos[axis], pos[3])
        return source, target

    def remote(stage, k, f, p, m):
        step = (*steps, 0)[m]
        source, target = ends(stage, k, f, p, step)
        return pltpu.make_async_remote_copy(
            src_ref=source,
            dst_ref=target,
            send_sem=send_sem.at[stage, k, f, p, m],
            recv_sem=recv_sem.at[stage, k, f, p, m],
            device_id=device_at(pos, (p + stage) % 3, step, stage == 2 and f == 1),
            device_id_type=MESH,
        )

    def copies(stage, k, f, p):
        if stage == 2 and f == 1:
            return [remote(stage, k, f, p, m) for m in range(4)], []
        source, target = ends(stage, k, f, p, 0)
        return (
            [remote(stage, k, f, p, m) for m in range(3)],
            [pltpu.make_async_copy(source, target, own_sem.at[stage, k, f, p])],
        )

    def start(*job):
        for group in copies(*job):
            for copy in group:
                copy.start()

    def arrive(*job):
        remotes, locals_ = copies(*job)
        for copy in remotes:
            copy.wait_recv()
        for copy in locals_:
            copy.wait()

    jobs = [
        (k, f, p)
        for f in (1, 0)
        for p in range(PARTS)
        for k in range(n)
        if p < firsts[k].shape[0]
    ]
    for job in jobs:
        start(0, *job)
    for stage in (1, 2):
        for job in jobs:
            arrive(stage - 1, *job)
            start(stage, *job)
    for job in jobs:
        arrive(2, *job)
    for stage in range(3):
        for job in jobs:
            for copy in copies(stage, *job)[0]:
                copy.wait_send()


def exchange(arrays, plans, collective_id, name):
    n = len(arrays)
    outs, temps = [], []
    for a, (src_places, dst_places) in zip(arrays, plans):
        front = [0] * 4
        for axis in range(4):
            front[dst_places[axis]] = a.shape[src_places[axis]]
        rest = a.shape[4:]
        outs.append(jax.ShapeDtypeStruct((*front, *rest), a.dtype))
        temps.append(pltpu.VMEM((rest[0],) + a.shape[:4] + rest[1:], a.dtype))
    anywhere = pl.BlockSpec(memory_space=pl.ANY)
    return pl.pallas_call(
        functools.partial(exchange_kernel, plans),
        name=name,
        out_shape=outs,
        in_specs=[anywhere] * n,
        out_specs=[anywhere] * n,
        scratch_shapes=temps
        + temps
        + [pltpu.SemaphoreType.DMA((3, n, 2, PARTS, 4))] * 2
        + [pltpu.SemaphoreType.DMA((3, n, 2, PARTS))],
        compiler_params=pltpu.CompilerParams(
            collective_id=collective_id, has_side_effects=True, vmem_limit_bytes=VMEM_BYTES
        ),
    )(*arrays)


def plan_kernel(grid, owner, tile, live, cell, turn, labels, left):
    n_grp, n_dev = grid
    devices = n_grp * n_dev
    chips = devices // 2

    @pl.loop(0, devices, unroll=8)
    def _(o):
        labels[o, 0] = -1
        labels[o, 1] = -1
        labels[o, 2] = 0

    @pl.loop(0, cell.shape[0], unroll=8)
    def _(e):
        cell[e] = -1
        turn[e] = 0

    def first(t, n):
        o = owner[t]
        e = lax.rem(o, 2) * chips + lax.div(o, 2)
        taken = cell[e] >= 0

        @pl.when(jnp.logical_not(taken))
        def _():
            cell[e] = t
            labels[o, 0] = tile[t]

        @pl.when(taken)
        def _():
            left[n] = t

        return n + taken.astype(jnp.int32)

    n_left = lax.fori_loop(0, live[0], first, jnp.int32(0))

    def insert(q, carry):
        lost, noise = carry

        def body(state):
            t, steps, noise = state
            o, k = owner[t], tile[t]
            x = lax.rem(k, n_grp) * n_dev + lax.div(k, n_grp)
            e0 = lax.rem(o, 2) * chips + lax.div(o, 2)
            e1 = devices + lax.div(o, 2)
            e2 = lax.rem(x, 2) * chips + lax.div(x, 2)
            e3 = devices + lax.div(x, 2)
            noise = lax.rem(noise * 1103 + 12345, 65521)
            pick = lax.rem(lax.div(noise, 8), 4)
            for r, e in ((3, e3), (2, e2), (0, e0), (1, e1)):
                pick = jnp.where(cell[e] < 0, r, pick)
            e = jnp.where(pick == 0, e0, jnp.where(pick == 1, e1, jnp.where(pick == 2, e2, e3)))
            turned = pick >= 2
            to = jnp.where(turned, x, o)
            label = jnp.where(turned, lax.rem(o, n_dev) * n_grp + lax.div(o, n_dev), k)
            victim = cell[e]
            cell[e] = t
            turn[e] = turned.astype(jnp.int32)
            both = (e >= devices).astype(jnp.int32)
            labels[to, both] = label

            @pl.when(e >= devices)
            def _():
                labels[to + 1 - 2 * lax.rem(to, 2), 1] = -1

            return victim, steps + 1, noise

        t, _, noise = lax.while_loop(
            lambda state: (state[0] >= 0) & (state[1] < WALK), body, (left[q], 0, noise)
        )
        return lost | (t >= 0).astype(jnp.int32), noise

    lost, _ = lax.fori_loop(0, n_left, insert, (jnp.int32(0), jnp.int32(1)))

    @pl.when(lost > 0)
    def _():
        @pl.loop(0, devices)
        def _(o):
            labels[o, 2] = 1


def make_plan(owner, tile, live, grid):
    devices = grid[0] * grid[1]
    smem = pl.BlockSpec(memory_space=pltpu.SMEM)
    cells = jax.ShapeDtypeStruct((devices * 3 // 2,), jnp.int32)
    return pl.pallas_call(
        functools.partial(plan_kernel, grid),
        name="plan",
        out_shape=[cells, cells, jax.ShapeDtypeStruct((devices, LANES), jnp.int32)],
        in_specs=[smem] * 3,
        out_specs=[smem] * 3,
        scratch_shapes=[pltpu.SMEM(tile.shape, jnp.int32)],
    )(owner, tile, live)


def fetch_copies(strength, here, in_sem):
    pieces = in_sem.shape[0]
    piece = strength.shape[1] // pieces
    return [
        pltpu.make_async_copy(
            strength.at[:, pl.ds(i * piece, piece)],
            here.at[:, pl.ds(i * piece, piece)],
            in_sem.at[i],
        )
        for i in range(pieces)
    ]


def turn_factors(fetches, freqs, here, turned, rows):
    _, bands, _, trip = here.shape
    flat = turned.reshape(2 * trip * bands, LANES)
    flat_rows = rows.reshape(2 * trip * 8, LANES)
    lines = []
    for mode in (0, 1):
        occ = 1.0 / (jnp.exp(freqs[mode]) - 1.0)
        lines.append((freqs[mode].T, jnp.sqrt(occ * (occ + 1.0)).T))
    for f in (0, 1):
        for q, value in enumerate(lines[f] + lines[1 - f]):
            flat_rows[pl.ds(f * trip * 8 + q, trip, stride=8), 0:bands] = value
    third = 1.0 / (jnp.exp(freqs[2]) - 1.0) + 1.0
    eye = (
        lax.broadcasted_iota(jnp.int32, (trip, trip), 0)
        == lax.broadcasted_iota(jnp.int32, (trip, trip), 1)
    ).astype(jnp.bfloat16)
    piece = bands // len(fetches)
    for i, fetch in enumerate(fetches):
        fetch.wait()

        @pl.loop(i * piece, (i + 1) * piece, unroll=10)
        def _(j):
            scaled = (here[0, j].astype(jnp.float32) * third).astype(jnp.bfloat16)
            flat[pl.ds(j, trip, stride=bands), 0:bands] = scaled.T.astype(jnp.float32)
            other = lax.dot_general(
                eye, here[1, j], (((1,), (1,)), ((), ())), preferred_element_type=jnp.float32
            )
            flat[pl.ds(trip * bands + j, trip, stride=bands), 0:bands] = other


def block_of(turned, rows, trip, bands, t, f):
    factors = [
        turned[h * trip + t][:, 0:bands].astype(jnp.bfloat16) for h in (f, 1 - f)
    ]
    core = lax.dot_general(
        *factors, (((1,), (1,)), ((), ())), preferred_element_type=jnp.float32
    )
    line = rows[f * trip + t]
    column = line.T[0:bands]
    diff = column[:, 0:1] - line[2:3, 0:bands]
    scale = column[:, 1:2] * line[3:4, 0:bands] * jnp.exp(-diff * diff / 0.5)
    value = jnp.pad(scale * core, ((0, 0), (0, LANES - bands)))
    return value.reshape(PARTS, bands // PARTS, LANES).astype(jnp.bfloat16)


def dense_kernel(
    grid, owner, tile, live, strength, freqs, out, labels,
    here, turned, rows, block, cell, place, in_sem, out_sem,
):
    _, bands, _, trip = strength.shape
    devices = grid[0] * grid[1]
    chips = devices // 2
    fetches = fetch_copies(strength, here, in_sem)
    for fetch in fetches:
        fetch.start()

    @pl.loop(0, devices)
    def _(o):
        labels[o, 0] = -1
        labels[o, 1] = -1
        cell[o] = 0

    @pl.loop(0, trip)
    def _(t):
        place[t] = -1

    @pl.loop(0, live[0])
    def _(t):
        o = owner[t]
        r = cell[o]
        cell[o] = r + 1
        place[t] = (r * 2 + lax.rem(o, 2)) * chips + lax.div(o, 2)
        labels[o, r] = tile[t]

    turn_factors(fetches, freqs, here, turned, rows)

    def send(t):
        return pltpu.make_async_copy(block.at[t], out.at[place[t]], out_sem)

    @pl.loop(0, trip)
    def _(t):
        block[t] = block_of(turned, rows, trip, bands, t, 0)

        @pl.when(place[t] >= 0)
        def _():
            send(t).start()

    @pl.loop(0, trip)
    def _(t):
        @pl.when(place[t] >= 0)
        def _():
            send(t).wait()


def dense_blocks(strength, freqs, owner, tile, live, grid):
    _, bands, _, trip = strength.shape
    devices = grid[0] * grid[1]
    smem = pl.BlockSpec(memory_space=pltpu.SMEM)
    anywhere = pl.BlockSpec(memory_space=pl.ANY)
    part = (PARTS, bands // PARTS, LANES)
    return pl.pallas_call(
        functools.partial(dense_kernel, grid),
        name="dense_blocks",
        out_shape=[
            jax.ShapeDtypeStruct((devices * 2, *part), jnp.bfloat16),
            jax.ShapeDtypeStruct((devices, LANES), jnp.int32),
        ],
        in_specs=[smem, smem, smem, anywhere, pl.BlockSpec(memory_space=pltpu.VMEM)],
        out_specs=[anywhere, smem],
        scratch_shapes=[
            pltpu.VMEM(strength.shape, strength.dtype),
            pltpu.VMEM((2 * trip, bands, LANES), jnp.float32),
            pltpu.VMEM((2 * trip, 8, LANES), jnp.float32),
            pltpu.VMEM((trip, *part), jnp.bfloat16),
            pltpu.SMEM((devices,), jnp.int32),
            pltpu.SMEM((trip,), jnp.int32),
            pltpu.SemaphoreType.DMA((PIECES,)),
            pltpu.SemaphoreType.DMA,
        ],
        compiler_params=pltpu.CompilerParams(vmem_limit_bytes=VMEM_BYTES),
    )(owner, tile, live, strength, freqs)


def send_blocks_kernel(
    cell, turn, strength, freqs, labels, own_out, labels_out, shared_out,
    here, turned, rows, staged, first, second, shared_in, labels_first, labels_second,
    in_sem, send_sem, recv_sem, own_sem, last_send, last_recv, last_own, labels_send, labels_recv, labels_own,
):
    _, bands, _, trip = strength.shape
    pos = position()
    steps = (1, 3, 2)
    slabs = (1, 3, 2, 0)
    fetches = fetch_copies(strength, here, in_sem)
    for fetch in fetches:
        fetch.start()

    barrier = pltpu.get_barrier_semaphore()
    greeted = [(a, r, f) for a in range(3) for r in (1, 2, 3) for f in (False, True)]
    greeted.append((0, 0, True))
    for a, r, f in greeted:
        pl.semaphore_signal(
            barrier, inc=1, device_id=device_at(pos, a, r, f), device_id_type=MESH
        )
    turn_factors(fetches, freqs, here, turned, rows)
    pl.semaphore_wait(barrier, len(greeted))

    def moved(axis, step):
        return lax.rem(pos[axis] + step, SIDE) if step else pos[axis]

    def compute(x):
        @pl.loop(0, 6)
        def _(i):
            k, half = lax.div(i, 2), lax.rem(i, 2)
            for u in range(8):
                e = k * SIDE**3 + x * SIDE**2 + half * 8 + u
                t = jnp.maximum(cell[e], 0)
                staged[k, x, half * 2 + u // SIDE, u % SIDE] = block_of(
                    turned, rows, trip, bands, t, turn[e]
                )

    def cut(ref, front, p, core, **at):
        index = [core] + [at.get(name, slice(None)) for name in "xyz"]
        return ref.at[(p, *index)] if front else ref.at[(*index, p)]

    def early(stage, p, q):
        axis = (p + stage) % 3
        source, target = ((staged, first), (first, second))[stage]

        def ends(step):
            if axis == 0:
                there, here_at = {"x": moved(0, step)}, {"x": pos[0]}
            else:
                r = slabs[q]
                x = moved(0, (SIDE - r) % SIDE if p == 0 else r)
                there = {"x": x, "xyz"[axis]: moved(axis, step)}
                here_at = {"x": x, "xyz"[axis]: pos[axis]}
            return (
                cut(source, stage > 0, p, slice(None), **there),
                cut(target, True, p, slice(None), **here_at),
            )

        def remote(m, step):
            source_at, target_at = ends(step)
            return pltpu.make_async_remote_copy(
                src_ref=source_at,
                dst_ref=target_at,
                send_sem=send_sem.at[stage, p, q, m],
                recv_sem=recv_sem.at[stage, p, q, m],
                device_id=device_at(pos, axis, step, False),
                device_id_type=MESH,
            )

        def local():
            return pltpu.make_async_copy(*ends(0), own_sem.at[stage, p, q])

        if axis == 0:
            return ([remote(0, slabs[q])], []) if slabs[q] else ([], [local()])
        return [remote(m, step) for m, step in enumerate(steps)], [local()]

    def late(p, f, m):
        axis = (p + 2) % 3
        step = (*steps, 0)[m]
        core = (pos[3], 1 - pos[3], 2)[f]
        there, here_at = {"xyz"[axis]: moved(axis, step)}, {"xyz"[axis]: pos[axis]}
        source = cut(second, True, p, core, **there)
        index = [here_at.get(name, slice(None)) for name in "xyz"]
        if f < 2:
            target = own_out.at[(*index, pos[3], p)]
        else:
            target = shared_in.at[(p, *index)]
        if step == 0 and f != 1:
            return pltpu.make_async_copy(source, target, last_own.at[p, f])
        return pltpu.make_async_remote_copy(
            src_ref=source,
            dst_ref=target,
            send_sem=last_send.at[p, f, m],
            recv_sem=last_recv.at[p, f, m],
            device_id=device_at(pos, axis, step, f == 1),
            device_id_type=MESH,
        )

    def is_local(f, m):
        return m == 3 and f != 1

    def pass_on(p):
        target = shared_out.at[:, :, :, pos[3], p]
        there = pltpu.make_async_remote_copy(
            src_ref=shared_in.at[p],
            dst_ref=target,
            send_sem=last_send.at[p, 3, 0],
            recv_sem=last_recv.at[p, 3, 0],
            device_id=device_at(pos, 0, 0, True),
            device_id_type=MESH,
        )
        return there, pltpu.make_async_copy(shared_in.at[p], target, last_own.at[p, 1])

    def label_messages(stage):
        source, target = (
            (labels, labels_first), (labels_first, labels_second), (labels_second, labels_out)
        )[stage]
        moves = [(r, f) for r in steps for f in (False, True)[: 1 + stage // 2]]
        moves += [(0, True)] if stage == 2 else []

        def ends(step, flip):
            at = [slice(None)] * 4
            to = [slice(None)] * 4
            at[stage], to[stage] = moved(stage, step), pos[stage]
            if stage == 2:
                at[3], to[3] = 1 - pos[3] if flip else pos[3], pos[3]
            return source.at[tuple(at)], target.at[tuple(to)]

        remotes = []
        for m, (step, flip) in enumerate(moves):
            source_at, target_at = ends(step, flip)
            remotes.append(
                pltpu.make_async_remote_copy(
                    src_ref=source_at,
                    dst_ref=target_at,
                    send_sem=labels_send.at[stage, m],
                    recv_sem=labels_recv.at[stage, m],
                    device_id=device_at(pos, stage, step, flip),
                    device_id_type=MESH,
                )
            )
        return remotes, [pltpu.make_async_copy(*ends(0, False), labels_own.at[stage])]

    def start(messages):
        for group in messages:
            for copy in group:
                copy.start()

    def arrive(messages):
        remotes, locals_ = messages
        for copy in remotes:
            copy.wait_recv()
        for copy in locals_:
            copy.wait()

    start(label_messages(0))
    for q in range(SIDE):
        compute(moved(0, slabs[q]))
        for p in range(PARTS):
            start(early(0, p, q))
    arrive(label_messages(0))
    start(label_messages(1))
    for q in range(SIDE):
        for p in range(PARTS):
            arrive(early(0, p, q))
            start(early(1, p, q))
    arrive(label_messages(1))
    start(label_messages(2))
    for q in range(SIDE):
        arrive(early(1, 1, q))
        m = (*steps, 0).index(slabs[q])
        for f in (2, 1, 0):
            late(1, f, m).start()
    for p in (0, 2):
        for q in range(SIDE):
            arrive(early(1, p, q))
        for f in (2, 1, 0):
            for m in range(4):
                late(p, f, m).start()
    arrive(label_messages(2))
    for f in (2, 1, 0):
        for p in (1, 0, 2):
            for m in range(4):
                if is_local(f, m):
                    late(p, f, m).wait()
                else:
                    late(p, f, m).wait_recv()
            if f == 2:
                for copy in pass_on(p):
                    copy.start()
    for p in range(PARTS):
        there, at_home = pass_on(p)
        there.wait()
        at_home.wait()
        for f in range(3):
            for m in range(4):
                if not is_local(f, m):
                    late(p, f, m).wait_send()
        for stage in range(2):
            for q in range(SIDE):
                for copy in early(stage, p, q)[0]:
                    copy.wait_send()
    for stage in range(3):
        for copy in label_messages(stage)[0]:
            copy.wait_send()


def send_blocks(cell, turn, labels, strength, freqs, collective_id):
    _, bands, _, trip = strength.shape
    part = (bands // PARTS, LANES)
    torus = (SIDE, SIDE, SIDE)
    moving = pltpu.VMEM((PARTS, 3, *torus, *part), jnp.bfloat16)
    arrived = jax.ShapeDtypeStruct((*torus, 2, PARTS, *part), jnp.bfloat16)
    smem = pl.BlockSpec(memory_space=pltpu.SMEM)
    anywhere = pl.BlockSpec(memory_space=pl.ANY)
    dma = pltpu.SemaphoreType.DMA
    return pl.pallas_call(
        send_blocks_kernel,
        name="send_blocks",
        out_shape=[arrived, jax.ShapeDtypeStruct(labels.shape, labels.dtype), arrived],
        in_specs=[smem, smem, anywhere, pl.BlockSpec(memory_space=pltpu.VMEM), anywhere],
        out_specs=[anywhere] * 3,
        scratch_shapes=[
            pltpu.VMEM(strength.shape, strength.dtype),
            pltpu.VMEM((2 * trip, bands, LANES), jnp.float32),
            pltpu.VMEM((2 * trip, 8, LANES), jnp.float32),
            pltpu.VMEM((3, *torus, PARTS, *part), jnp.bfloat16),
            moving,
            moving,
            pltpu.VMEM((PARTS, *torus, *part), jnp.bfloat16),
            pltpu.VMEM(labels.shape, labels.dtype),
            pltpu.VMEM(labels.shape, labels.dtype),
            dma((PIECES,)),
            dma((2, PARTS, SIDE, 3)),
            dma((2, PARTS, SIDE, 3)),
            dma((2, PARTS, SIDE)),
            dma((PARTS, 4, 4)),
            dma((PARTS, 4, 4)),
            dma((PARTS, 3)),
            dma((3, 7)),
            dma((3, 7)),
            dma((3,)),
        ],
        compiler_params=pltpu.CompilerParams(
            collective_id=collective_id, has_side_effects=True, vmem_limit_bytes=VMEM_BYTES
        ),
    )(cell, turn, strength, freqs, labels)


def sum_kernel(labels, one, two, out, total):
    step = pl.program_id(0)
    here = one.shape[0]
    tiles = out.shape[0]

    @pl.when(step == 0)
    def _():
        @pl.loop(0, tiles, unroll=4)
        def _(k):
            total[k] = jnp.zeros(total.shape[1:], jnp.float32)

    @pl.loop(0, here, unroll=4)
    def _(s):
        for r, got in enumerate((one, two)):
            label = labels[step * here + s, r]
            total[jnp.where(label < 0, tiles, label)] += got[s].astype(jnp.float32)

    @pl.when(step == pl.num_programs(0) - 1)
    def _():
        @pl.loop(0, tiles, unroll=4)
        def _(k):
            out[k] = total[k].astype(out.dtype)


def sum_tiles(labels, one, two, tiles):
    devices, *part = one.shape
    here = 32
    spec = pl.BlockSpec((here, *part), lambda i: (i, 0, 0, 0))
    return pl.pallas_call(
        sum_kernel,
        name="sum_tiles",
        grid=(devices // here,),
        out_shape=jax.ShapeDtypeStruct((tiles, *part), jnp.bfloat16),
        in_specs=[pl.BlockSpec(memory_space=pltpu.SMEM), spec, spec],
        out_specs=pl.BlockSpec(memory_space=pltpu.VMEM),
        scratch_shapes=[pltpu.VMEM((tiles + 1, *part), jnp.float32)],
        compiler_params=pltpu.CompilerParams(vmem_limit_bytes=VMEM_BYTES),
    )(labels, one, two)


def symmetrize_kernel(n_grp, omega, partner, out):
    per, thirds, part, lanes = omega.shape
    bands = thirds * part
    for k in range(per):
        turned = partner[k].astype(jnp.float32).reshape(bands, lanes).T
        mine = omega[k].astype(jnp.float32).reshape(bands, lanes)
        i, c = divmod(k, n_grp)
        out[i, pl.ds(c, bands, stride=n_grp), :] = 0.5 * (mine[:, 0:bands] + turned[0:bands])


def symmetrize(omega, partner, n_grp):
    tiles, thirds, part, lanes = omega.shape
    bands = thirds * part
    rows = 8
    spec = pl.BlockSpec((rows * n_grp, thirds, part, lanes), lambda i: (i, 0, 0, 0))
    return pl.pallas_call(
        functools.partial(symmetrize_kernel, n_grp),
        name="symmetrize",
        grid=(tiles // (rows * n_grp),),
        out_shape=jax.ShapeDtypeStruct((tiles // n_grp, bands * n_grp, bands), jnp.float32),
        in_specs=[spec, spec],
        out_specs=pl.BlockSpec((rows, bands * n_grp, bands), lambda i: (i, 0, 0)),
        compiler_params=pltpu.CompilerParams(vmem_limit_bytes=VMEM_BYTES),
    )(omega, partner)


def per_device(strength, freqs, owner, tile_slot, live_count):
    bands = strength.shape[2]
    n_grp = lax.axis_size("grp")
    n_dev = lax.axis_size("dev")
    grid = (n_grp, n_dev)
    devices = n_grp * n_dev
    part = (PARTS, bands // PARTS, LANES)
    torus = (SIDE, SIDE, SIDE)
    plain = ((0, 1, 2, 3), (0, 1, 2, 3))
    by_lane, freqs = strength.transpose(1, 2, 3, 0), freqs.transpose(1, 2, 0)
    names = (owner[:, 0], tile_slot, live_count)

    def with_labels(labels):
        return labels.reshape(*torus, 2, 1, 1, LANES)

    cell, turn, labels = make_plan(*names, grid)
    own, labels, shared = send_blocks(cell, turn, with_labels(labels), by_lane, freqs, 1)
    labels = labels.reshape(devices, LANES)

    def sum_shared():
        return sum_tiles(
            labels, own.reshape(devices, *part), shared.reshape(devices, *part), devices
        )

    def sum_dense():
        cells, labels = dense_blocks(by_lane, freqs, *names, grid)
        cells = cells.reshape(2, 2, *torus, *part)
        moved = ((1, 2, 3, 0), (0, 1, 2, 3))
        one, two, labels = exchange(
            [cells[0], cells[1], with_labels(labels)], [moved, moved, plain], 3, "send_dense"
        )
        return sum_tiles(
            labels.reshape(devices, LANES),
            one.reshape(devices, *part),
            two.reshape(devices, *part),
            devices,
        )

    omega = lax.cond(jnp.any(labels[:, 2] > 0), sum_dense, sum_shared)
    by_dev = ((3, 0, 1, 2), (3, 0, 1, 2))
    (partner,) = exchange(
        [omega.reshape(SIDE, SIDE, 2, n_grp, *part)], [by_dev], 2, "send_tiles"
    )
    sym = symmetrize(omega, partner.reshape(omega.shape), n_grp)
    return sym.reshape(devices // n_grp, bands, n_grp, 1, bands)


def solution(mesh):
    return jax.shard_map(
        per_device,
        mesh=mesh,
        in_specs=(
            P(("grp", "dev"), None, None, None),
            P(("grp", "dev"), None, None),
            P(("grp", "dev"), None),
            P(("grp", "dev")),
            P(("grp", "dev")),
        ),
        out_specs=P("grp", None, None, "dev", None),
        check_vma=False,
    )
```

time: 177 us -> 163 us (0.921)
  Pallas kernels: 172 us -> 158 us
    pallas_call x2 -> x1, Pallas kernels: 137 us -> 53.3 us  [exchange(): pl.pallas_call(functools.partial(exchange_kernel, plans), name=name, out_...]
    pallas_call x1 -> x2, Pallas kernels: 21.3 us -> 90.4 us  [the longest x1 84.8 us: send_blocks(): pl.pallas_call(send_blocks_kernel, name='send_blocks', out_shape=[arrived...]
where the time goes in v4:
time: 163 us; the launch traced here: 160 us
  Pallas kernels  158 us (97%)
    pallas_call x1, Pallas kernels, send_blocks(): pl.pallas_call(send_blocks_kernel, name='send_blocks', out_shape=[arrived...  84.8 us
    pallas_call x1, Pallas kernels, exchange(): pl.pallas_call(functools.partial(exchange_kernel, plans), name=name, out_...  53.3 us
    pallas_call x1, Pallas kernels, sum_tiles(): pl.pallas_call(sum_kernel, name='sum_tiles', grid=(devices // here,), out...  7.88 us
    pallas_call x1, Pallas kernels, symmetrize(): pl.pallas_call(functools.partial(symmetrize_kernel, n_grp), name='symmetr...  6.13 us
    pallas_call x1, Pallas kernels, make_plan(): pl.pallas_call(functools.partial(plan_kernel, grid), name='plan', out_sha...  5.68 us

profile of v4, /device:TPU:11, one launch (start us, length us, event | category | flops | bytes accessed | tf_op | source)
XLA Modules:
  0.0 159.9 jit_solution(4050788979261505775)
XLA Ops:
  0.0 0.0 copy-start.3
  0.0 0.0 copy-start.2
  0.0 0.0 copy-start.1
  0.7 5.7 %plan.1 = (s32[192]{0:T(256)}, s32[192]{0:T(256)}, s32[128,128]{1,0:T(8,128)}) custom-call(s32[128]{0:T(128)} %bitcast.35, s32[128]{0:T(128)} %tile.1, s32[1]{0:T(128)S(6)} %copy.9.live), custom_call_target="tpu_custom_call" | custom-call | tf_op jit(solution)/shard_map/plan/pallas_call | solution.py:233
  6.4 84.8 %send_blocks.1 = (bf16[4,4,4,2,3,40,128]{6,5,4,3,2,1,0:T(8,128)(2,1)}, s32[4,4,4,2,1,1,128]{6,5,4,3,2,1,0:T(1,128)S(1)}, bf16[4,4,4,2,3,40,128]{6,5,4,3,2,1,0:T(8,128)(2,1)}) custom-call(s32[192]{0:T(256)} %get-tuple-element.43.cell, s32[192]{0:T(256)} %get-tuple-element.44.turn, bf16[2,120,120,128]{3,2,1,0:T(8,128)(2,1)} %bitcast.19, ...), custom_call_target="tpu_custom_call" | custom-call | tf_op jit(solution)/shard_map/send_blocks/pallas_call | solution.py:595
  91.2 0.7 fusion
  92.5 0.0 copy-done.3
  92.5 0.0 copy-done.2
  92.6 0.0 copy-done.1
  92.6 7.9 %conditional.1 = (bf16[128,3,40,128]{3,2,1,0:T(8,128)(2,1)}) conditional(s32[]{:T(128)} %convert_element_type.3, (bf16[4,4,4,2,3,40,128]{6,5,4,3,2,1,0:T(8,128)(2,1)}, bf16[4,4,4,2,3,40,128]{6,5,4,3,2,1,0:T(8,128)(2,1)}, s32[128,128]{1,0:T(8,128)S(1)}) %tuple.18, (s32[128]{0:T(128)S(1)}, s32[128]{0:T(128)S(1)}, s32[1]{0:T(128)}, ...), branch_computations={%region_1.0_spmd, %region_2.0_spmd} | conditional | bytes 15728648 | solution.py:732
  92.6 7.9 %sum_tiles.2 = bf16[128,3,40,128]{3,2,1,0:T(8,128)(2,1)} custom-call(s32[128,128]{1,0:T(8,128)S(1)} %get-tuple-element.24.labels, bf16[128,3,40,128]{3,2,1,0:T(8,128)(2,1)} %bitcast.24, bf16[128,3,40,128]{3,2,1,0:T(8,128)(2,1)} %bitcast.25), custom_call_target="tpu_custom_call" | custom-call | tf_op jit(solution)/shard_map/cond/branch_0_fun/sum_tiles/pallas_call | solution.py:656
  100.5 0.0 copy-start
  100.5 53.3 %send_tiles.1 = bf16[4,4,2,4,3,40,128]{6,5,4,3,2,1,0:T(8,128)(2,1)} custom-call(bf16[4,4,2,4,3,40,128]{6,5,4,3,2,1,0:T(8,128)(2,1)} %bitcast.18), custom_call_target="tpu_custom_call" | custom-call | tf_op jit(solution)/shard_map/send_tiles/pallas_call | solution.py:134
  153.8 0.0 copy-done
  153.8 6.1 %symmetrize.1 = f32[32,480,120]{2,1,0:T(8,128)} custom-call(bf16[128,3,40,128]{3,2,1,0:T(8,128)(2,1)S(1)} %copy-done, bf16[128,3,40,128]{3,2,1,0:T(8,128)(2,1)} %bitcast.23), custom_call_target="tpu_custom_call" | custom-call | tf_op jit(solution)/shard_map/symmetrize/pallas_call | solution.py:683
Async XLA Ops:
  0.0 92.5 %copy-start.3 = (s32[128]{0:T(128)S(1)}, s32[128]{0:T(128)}, u32[]{:S(2)}) copy-start(s32[128]{0:T(128)} %tile.1) | copy-start | bytes 1540
  0.0 92.5 %copy-start.2 = (s32[128,1]{0,1:T(1,128)S(1)}, s32[128,1]{0,1:T(1,128)}, u32[]{:S(2)}) copy-start(s32[128,1]{0,1:T(1,128)} %param.9) | copy-start | bytes 1540
  0.0 92.5 %copy-start.1 = (f32[128,3,120]{0,2,1:T(8,128)S(1)}, f32[128,3,120]{0,2,1:T(8,128)}, u32[]{:S(2)}) copy-start(f32[128,3,120]{0,2,1:T(8,128)} %param.8) | copy-start | bytes 552964
  100.5 53.3 %copy-start = (bf16[128,3,40,128]{3,2,1,0:T(8,128)(2,1)S(1)}, bf16[128,3,40,128]{3,2,1,0:T(8,128)(2,1)}, u32[]{:S(2)}) copy-start(bf16[128,3,40,128]{3,2,1,0:T(8,128)(2,1)} %get-tuple-element.51.omega) | copy-start | bytes 11796484

commit v5 on v4

--- a/solution.py
+++ b/solution.py
@@ -15,7 +15,7 @@
 
 PARTS = 3
 WALK = 400
-PIECES = 6
+PIECES = 12
 
 
 def position():
@@ -154,9 +154,8 @@
 
     @pl.loop(0, devices, unroll=8)
     def _(o):
-        labels[o, 0] = -1
-        labels[o, 1] = -1
-        labels[o, 2] = 0
+        labels[0, o] = -1
+        labels[1, o] = -1
 
     @pl.loop(0, cell.shape[0], unroll=8)
     def _(e):
@@ -166,17 +165,11 @@
     def first(t, n):
         o = owner[t]
         e = lax.rem(o, 2) * chips + lax.div(o, 2)
-        taken = cell[e] >= 0
-
-        @pl.when(jnp.logical_not(taken))
-        def _():
-            cell[e] = t
-            labels[o, 0] = tile[t]
-
-        @pl.when(taken)
-        def _():
-            left[n] = t
-
+        held = cell[e]
+        taken = held >= 0
+        cell[e] = jnp.where(taken, held, t)
+        labels[0, o] = jnp.where(taken, labels[0, o], tile[t])
+        left[n] = t
         return n + taken.astype(jnp.int32)
 
     n_left = lax.fori_loop(0, live[0], first, jnp.int32(0))
@@ -204,11 +197,11 @@
             cell[e] = t
             turn[e] = turned.astype(jnp.int32)
             both = (e >= devices).astype(jnp.int32)
-            labels[to, both] = label
+            labels[both, to] = label
 
             @pl.when(e >= devices)
             def _():
-                labels[to + 1 - 2 * lax.rem(to, 2), 1] = -1
+                labels[1, to + 1 - 2 * lax.rem(to, 2)] = -1
 
             return victim, steps + 1, noise
 
@@ -219,11 +212,7 @@
 
     lost, _ = lax.fori_loop(0, n_left, insert, (jnp.int32(0), jnp.int32(1)))
 
-    @pl.when(lost > 0)
-    def _():
-        @pl.loop(0, devices)
-        def _(o):
-            labels[o, 2] = 1
+    labels[2, 0] = lost
 
 
 def make_plan(owner, tile, live, grid):
@@ -233,10 +222,10 @@
     return pl.pallas_call(
         functools.partial(plan_kernel, grid),
         name="plan",
-        out_shape=[cells, cells, jax.ShapeDtypeStruct((devices, LANES), jnp.int32)],
+        out_shape=[cells, cells, jax.ShapeDtypeStruct((3, devices), jnp.int32)],
         in_specs=[smem] * 3,
         out_specs=[smem] * 3,
-        scratch_shapes=[pltpu.SMEM(tile.shape, jnp.int32)],
+        scratch_shapes=[pltpu.SMEM((tile.shape[0] + 1,), jnp.int32)],
     )(owner, tile, live)
 
 
@@ -255,7 +244,7 @@
 
 def turn_factors(fetches, freqs, here, turned, rows):
     _, bands, _, trip = here.shape
-    flat = turned.reshape(2 * trip * bands, LANES)
+    flat = turned.reshape(turned.shape[0] * bands, LANES)
     flat_rows = rows.reshape(2 * trip * 8, LANES)
     lines = []
     for mode in (0, 1):
@@ -376,10 +365,12 @@
     )(owner, tile, live, strength, freqs)
 
 
-def send_blocks_kernel(
-    cell, turn, strength, freqs, labels, own_out, labels_out, shared_out,
-    here, turned, rows, staged, first, second, shared_in, labels_first, labels_second,
+def main_kernel(
+    cell, turn, names, strength, freqs, omega_out, partner_out, flag,
+    here, turned, rows, staged, first, second, got_same, got_other, got_shared, tile_first, tile_second,
+    labels, labels_first, labels_second, labels_third, known, table, listed,
     in_sem, send_sem, recv_sem, own_sem, last_send, last_recv, last_own, labels_send, labels_recv, labels_own,
+    tile_send, tile_recv, tile_own, small_sem,
 ):
     _, bands, _, trip = strength.shape
     pos = position()
@@ -397,6 +388,15 @@
             barrier, inc=1, device_id=device_at(pos, a, r, f), device_id_type=MESH
         )
     turn_factors(fetches, freqs, here, turned, rows)
+    lane = lax.broadcasted_iota(jnp.int32, (1, LANES), 1)
+
+    @pl.loop(0, 2 * SIDE**3, unroll=8)
+    def _(o):
+        known_here = jnp.where(lane == 0, names[0, o], jnp.where(lane == 1, names[1, o], names[2, 0]))
+        labels[lax.div(o, 32), lax.rem(lax.div(o, 8), 4), lax.rem(lax.div(o, 2), 4), lax.rem(o, 2), 0] = (
+            known_here
+        )
+
     pl.semaphore_wait(barrier, len(greeted))
 
     def moved(axis, step):
@@ -460,9 +460,9 @@
         source = cut(second, True, p, core, **there)
         index = [here_at.get(name, slice(None)) for name in "xyz"]
         if f < 2:
-            target = own_out.at[(*index, pos[3], p)]
+            target = (got_same, got_other)[f].at[(*index, p)]
         else:
-            target = shared_in.at[(p, *index)]
+            target = got_shared.at[(*index, pos[3], p)]
         if step == 0 and f != 1:
             return pltpu.make_async_copy(source, target, last_own.at[p, f])
         return pltpu.make_async_remote_copy(
@@ -478,20 +478,19 @@
         return m == 3 and f != 1
 
     def pass_on(p):
-        target = shared_out.at[:, :, :, pos[3], p]
-        there = pltpu.make_async_remote_copy(
-            src_ref=shared_in.at[p],
-            dst_ref=target,
+        mine = got_shared.at[:, :, :, pos[3], p]
+        return pltpu.make_async_remote_copy(
+            src_ref=mine,
+            dst_ref=mine,
             send_sem=last_send.at[p, 3, 0],
             recv_sem=last_recv.at[p, 3, 0],
             device_id=device_at(pos, 0, 0, True),
             device_id_type=MESH,
         )
-        return there, pltpu.make_async_copy(shared_in.at[p], target, last_own.at[p, 1])
 
     def label_messages(stage):
         source, target = (
-            (labels, labels_first), (labels_first, labels_second), (labels_second, labels_out)
+            (labels, labels_first), (labels_first, labels_second), (labels_second, labels_third)
         )[stage]
         moves = [(r, f) for r in steps for f in (False, True)[: 1 + stage // 2]]
         moves += [(0, True)] if stage == 2 else []
@@ -530,6 +529,112 @@
             copy.wait_recv()
         for copy in locals_:
             copy.wait()
+
+    def order_labels():
+        copy = pltpu.make_async_copy(labels_third, known, small_sem)
+        copy.start()
+        copy.wait()
+        sources = 2 * SIDE**3
+        n = 2 * sources
+        lanes = lax.broadcasted_iota(jnp.int32, (8, n), 1)
+
+        def gather(s, carry):
+            keys, bad = carry
+            core = lax.rem(s, 2)
+            at = (lax.div(s, 32), lax.rem(lax.div(s, 8), 4), lax.rem(lax.div(s, 2), 4), core, 0, 0)
+            for r in range(2):
+                label = known[(*at, r)]
+                label = jnp.where(label < 0, sources, label)
+                if r == 0:
+                    label = label + jnp.where(core == pos[3], 2, 1) * (sources + 1)
+                keys = jnp.where(lanes == s + r * sources, label, keys)
+            return keys, jnp.maximum(bad, known[(*at, 2)])
+
+        names_row, bad = lax.fori_loop(
+            0, sources, gather, (jnp.zeros((8, n), jnp.int32), jnp.int32(0)), unroll=8
+        )
+        flag[0] = bad
+        row = lax.broadcasted_iota(jnp.int32, (n, n), 0)
+        column = lax.broadcasted_iota(jnp.int32, (n, n), 1)
+        keys = names_row * n + lanes
+        keys_down = keys.T[:, 0:1]
+        names_down = names_row.T[:, 0:1]
+
+        def count(mask):
+            return jnp.sum(mask.astype(jnp.int32), axis=0, keepdims=True)
+
+        ahead = keys_down < keys[0:1]
+        rank = count(ahead)
+        earlier = jnp.minimum(count(ahead & (names_down == names_row[0:1])), 1)
+        both = jnp.concatenate([rank, earlier] + [rank] * 6, axis=0).T
+        found = both[:, 0:1] == column
+        index = jnp.where(row < sources, lax.shift_right_logical(row, 1), row - sources)
+        table[0:1, :] = jnp.sum(jnp.where(found, index, 0), axis=0, keepdims=True)
+        table[1:2, :] = jnp.sum(jnp.where(found, both[:, 1:2], 0), axis=0, keepdims=True)
+        for g in range(3):
+            name = column + g * (sources + 1)
+            end = count(names_down <= name)
+            begin = count(names_down < name)
+            table[2 + g : 3 + g, :] = jnp.where(end > begin, end - 1, n)
+        copy = pltpu.make_async_copy(table, listed, small_sem)
+        copy.start()
+        copy.wait()
+
+    n_slots = 4 * SIDE**3
+    sums = turned.reshape(n_slots + 1, PARTS, bands // PARTS, LANES)
+
+    def sum_group(got, begin, end):
+        def add(r, total):
+            kept = listed[1, r].astype(jnp.float32)
+            at = listed[0, r]
+            index = []
+            for length in reversed(got.shape[:-3]):
+                index.insert(0, jnp.bitwise_and(at, length - 1))
+                at = lax.shift_right_logical(at, length.bit_length() - 1)
+            total = total * kept + got[tuple(index)].astype(jnp.float32)
+            sums[r] = total
+            return total
+
+        lax.fori_loop(begin, end, add, jnp.zeros(sums.shape[1:], jnp.float32), unroll=4)
+
+    def sum_part(p):
+        @pl.loop(0, n_slots // 2, unroll=8)
+        def _(k):
+            total = sums[listed[2, k], p] + sums[listed[3, k], p] + sums[listed[4, k], p]
+            x, d = lax.rem(k, SIDE), lax.div(k, SIDE)
+            staged[lax.rem(d, 2), x, lax.div(d, 8), lax.rem(lax.div(d, 2), SIDE), p] = (
+                total.astype(staged.dtype)
+            )
+
+    def tile_messages(stage, p, f):
+        axis = (p + stage) % 3
+        core = 1 - pos[3] if f else pos[3]
+
+        def ends(step):
+            there, here_at = {"xyz"[axis]: moved(axis, step)}, {"xyz"[axis]: pos[axis]}
+            source = cut((staged, tile_first, tile_second)[stage], stage > 0, p, core, **there)
+            if stage < 2:
+                return source, cut((tile_first, tile_second)[stage], True, p, core, **here_at)
+            index = [here_at.get(name, slice(None)) for name in "xyz"]
+            return source, partner_out.at[(*index, pos[3], p)]
+
+        crossing = stage == 2 and f == 1
+        remotes = []
+        for m, step in enumerate((*steps, 0) if crossing else steps):
+            source, target = ends(step)
+            remotes.append(
+                pltpu.make_async_remote_copy(
+                    src_ref=source,
+                    dst_ref=target,
+                    send_sem=tile_send.at[stage, p, f, m],
+                    recv_sem=tile_recv.at[stage, p, f, m],
+                    device_id=device_at(pos, axis, step, crossing),
+                    device_id_type=MESH,
+                )
+            )
+        if crossing:
+            return remotes, []
+        return remotes, [pltpu.make_async_copy(*ends(0), tile_own.at[stage, p, f])]
 
     start(label_messages(0))
     for q in range(SIDE):
@@ -556,58 +661,103 @@
             for m in range(4):
                 late(p, f, m).start()
     arrive(label_messages(2))
-    for f in (2, 1, 0):
-        for p in (1, 0, 2):
-            for m in range(4):
-                if is_local(f, m):
-                    late(p, f, m).wait()
-                else:
-                    late(p, f, m).wait_recv()
-            if f == 2:
-                for copy in pass_on(p):
-                    copy.start()
+    order_labels()
+    sums[n_slots] = jnp.zeros(sums.shape[1:], jnp.float32)
+
+    def arrive_late(p, f):
+        for m in range(4):
+            if is_local(f, m):
+                late(p, f, m).wait()
+            else:
+                late(p, f, m).wait_recv()
+
+    for p in (1, 0, 2):
+        arrive_late(p, 2)
+        pass_on(p).start()
+    for p in (1, 0, 2):
+        arrive_late(p, 1)
+    sum_group(got_other, n_slots // 2, n_slots * 3 // 4)
+    for p in (1, 0, 2):
+        pass_on(p).wait_recv()
+    sum_group(got_shared, 0, n_slots // 2)
+    for stage in range(2):
+        for p in range(PARTS):
+            for q in range(SIDE):
+                for copy in early(stage, p, q)[0]:
+                    copy.wait_send()
+    for p in (1, 0, 2):
+        arrive_late(p, 0)
+    sum_group(got_same, n_slots * 3 // 4, n_slots)
+    tile_jobs = [(p, f) for p in (1, 0, 2) for f in (1, 0)]
+    for p in (1, 0, 2):
+        sum_part(p)
+        for f in (1, 0):
+            start(tile_messages(0, p, f))
+    keep = pltpu.make_async_copy(staged.at[0:2], omega_out, small_sem)
+    keep.start()
+    for stage in (1, 2):
+        for job in tile_jobs:
+            arrive(tile_messages(stage - 1, *job))
+            start(tile_messages(stage, *job))
     for p in range(PARTS):
-        there, at_home = pass_on(p)
-        there.wait()
-        at_home.wait()
+        pass_on(p).wait_send()
         for f in range(3):
             for m in range(4):
                 if not is_local(f, m):
                     late(p, f, m).wait_send()
-        for stage in range(2):
-            for q in range(SIDE):
-                for copy in early(stage, p, q)[0]:
-                    copy.wait_send()
     for stage in range(3):
         for copy in label_messages(stage)[0]:
             copy.wait_send()
-
-
-def send_blocks(cell, turn, labels, strength, freqs, collective_id):
+    for job in tile_jobs:
+        arrive(tile_messages(2, *job))
+    keep.wait()
+    for stage in range(3):
+        for job in tile_jobs:
+            for copy in tile_messages(stage, *job)[0]:
+                copy.wait_send()
+
+
+def sums_and_partners(cell, turn, labels, strength, freqs, collective_id):
     _, bands, _, trip = strength.shape
     part = (bands // PARTS, LANES)
     torus = (SIDE, SIDE, SIDE)
     moving = pltpu.VMEM((PARTS, 3, *torus, *part), jnp.bfloat16)
-    arrived = jax.ShapeDtypeStruct((*torus, 2, PARTS, *part), jnp.bfloat16)
+    moving_tiles = pltpu.VMEM((PARTS, 2, *torus, *part), jnp.bfloat16)
     smem = pl.BlockSpec(memory_space=pltpu.SMEM)
     anywhere = pl.BlockSpec(memory_space=pl.ANY)
+    label_rows = (*torus, 2, 1, 1, LANES)
+    moving_labels = pltpu.VMEM(label_rows, jnp.int32)
     dma = pltpu.SemaphoreType.DMA
+    slots = 4 * SIDE**3
     return pl.pallas_call(
-        send_blocks_kernel,
-        name="send_blocks",
-        out_shape=[arrived, jax.ShapeDtypeStruct(labels.shape, labels.dtype), arrived],
-        in_specs=[smem, smem, anywhere, pl.BlockSpec(memory_space=pltpu.VMEM), anywhere],
-        out_specs=[anywhere] * 3,
+        main_kernel,
+        name="sums_and_partners",
+        out_shape=[
+            jax.ShapeDtypeStruct((2, *torus, PARTS, *part), jnp.bfloat16),
+            jax.ShapeDtypeStruct((*torus, 2, PARTS, *part), jnp.bfloat16),
+            jax.ShapeDtypeStruct((1,), jnp.int32),
+        ],
+        in_specs=[smem, smem, smem, anywhere, pl.BlockSpec(memory_space=pltpu.VMEM)],
+        out_specs=[anywhere, anywhere, smem],
         scratch_shapes=[
             pltpu.VMEM(strength.shape, strength.dtype),
-            pltpu.VMEM((2 * trip, bands, LANES), jnp.float32),
+            pltpu.VMEM((2 * trip + 1, bands, LANES), jnp.float32),
             pltpu.VMEM((2 * trip, 8, LANES), jnp.float32),
             pltpu.VMEM((3, *torus, PARTS, *part), jnp.bfloat16),
             moving,
             moving,
-            pltpu.VMEM((PARTS, *torus, *part), jnp.bfloat16),
-            pltpu.VMEM(labels.shape, labels.dtype),
-            pltpu.VMEM(labels.shape, labels.dtype),
+            pltpu.VMEM((*torus, PARTS, *part), jnp.bfloat16),
+            pltpu.VMEM((*torus, PARTS, *part), jnp.bfloat16),
+            pltpu.VMEM((*torus, 2, PARTS, *part), jnp.bfloat16),
+            moving_tiles,
+            moving_tiles,
+            moving_labels,
+            moving_labels,
+            moving_labels,
+            moving_labels,
+            pltpu.SMEM(label_rows, jnp.int32),
+            pltpu.VMEM((8, slots), jnp.int32),
+            pltpu.SMEM((8, slots), jnp.int32),
             dma((PIECES,)),
             dma((2, PARTS, SIDE, 3)),
             dma((2, PARTS, SIDE, 3)),
@@ -618,11 +768,15 @@
             dma((3, 7)),
             dma((3, 7)),
             dma((3,)),
+            dma((3, PARTS, 2, 4)),
+            dma((3, PARTS, 2, 4)),
+            dma((3, PARTS, 2)),
+            dma,
         ],
         compiler_params=pltpu.CompilerParams(
-            collective_id=collective_id, has_side_effects=True, vmem_limit_bytes=VMEM_BYTES
+            collective_id=collective_id, has_side_effects=True, vmem_limit_bytes=60 * 2**20
         ),
-    )(cell, turn, strength, freqs, labels)
+    )(cell, turn, labels, strength, freqs)
 
 
 def sum_kernel(labels, one, two, out, total):
@@ -665,29 +819,35 @@
     )(labels, one, two)
 
 
-def symmetrize_kernel(n_grp, omega, partner, out):
-    per, thirds, part, lanes = omega.shape
+def symmetrize_kernel(omega, partner, out):
+    *_, thirds, part, lanes = omega.shape
     bands = thirds * part
-    for k in range(per):
-        turned = partner[k].astype(jnp.float32).reshape(bands, lanes).T
-        mine = omega[k].astype(jnp.float32).reshape(bands, lanes)
-        i, c = divmod(k, n_grp)
-        out[i, pl.ds(c, bands, stride=n_grp), :] = 0.5 * (mine[:, 0:bands] + turned[0:bands])
-
-
-def symmetrize(omega, partner, n_grp):
-    tiles, thirds, part, lanes = omega.shape
+    for z in range(SIDE):
+        for core in range(2):
+            for x in range(SIDE):
+                mine = omega[core, x, 0, z].astype(jnp.float32).reshape(bands, lanes)
+                other = partner[x, 0, z, core].astype(jnp.float32).reshape(bands, lanes).T
+                out[z * 2 + core, pl.ds(x, bands, stride=SIDE), :] = 0.5 * (
+                    mine[:, 0:bands] + other[0:bands]
+                )
+
+
+def symmetrize(omega, partner):
+    *_, thirds, part, lanes = omega.shape
     bands = thirds * part
-    rows = 8
-    spec = pl.BlockSpec((rows * n_grp, thirds, part, lanes), lambda i: (i, 0, 0, 0))
+    rest = (thirds, part, lanes)
+    rows = 2 * SIDE
     return pl.pallas_call(
-        functools.partial(symmetrize_kernel, n_grp),
+        symmetrize_kernel,
         name="symmetrize",
-        grid=(tiles // (rows * n_grp),),
-        out_shape=jax.ShapeDtypeStruct((tiles // n_grp, bands * n_grp, bands), jnp.float32),
-        in_specs=[spec, spec],
-        out_specs=pl.BlockSpec((rows, bands * n_grp, bands), lambda i: (i, 0, 0)),
-        compiler_params=pltpu.CompilerParams(vmem_limit_bytes=VMEM_BYTES),
+        grid=(SIDE,),
+        out_shape=jax.ShapeDtypeStruct((rows * SIDE, bands * SIDE, bands), jnp.float32),
+        in_specs=[
+            pl.BlockSpec((2, SIDE, 1, SIDE, *rest), lambda y: (0, 0, y, 0, 0, 0, 0)),
+            pl.BlockSpec((SIDE, 1, SIDE, 2, *rest), lambda y: (0, y, 0, 0, 0, 0, 0)),
+        ],
+        out_specs=pl.BlockSpec((rows, bands * SIDE, bands), lambda y: (y, 0, 0)),
+        compiler_params=pltpu.CompilerParams(vmem_limit_bytes=60 * 2**20),
     )(omega, partner)
 
 
@@ -707,34 +867,31 @@
         return labels.reshape(*torus, 2, 1, 1, LANES)
 
     cell, turn, labels = make_plan(*names, grid)
-    own, labels, shared = send_blocks(cell, turn, with_labels(labels), by_lane, freqs, 1)
-    labels = labels.reshape(devices, LANES)
-
-    def sum_shared():
-        return sum_tiles(
-            labels, own.reshape(devices, *part), shared.reshape(devices, *part), devices
-        )
-
-    def sum_dense():
+    omega, partner, flag = sums_and_partners(
+        cell, turn, labels, by_lane, freqs, 1
+    )
+
+    def main():
+        return symmetrize(omega, partner)
+
+    def dense():
         cells, labels = dense_blocks(by_lane, freqs, *names, grid)
         cells = cells.reshape(2, 2, *torus, *part)
         moved = ((1, 2, 3, 0), (0, 1, 2, 3))
         one, two, labels = exchange(
             [cells[0], cells[1], with_labels(labels)], [moved, moved, plain], 3, "send_dense"
         )
-        return sum_tiles(
+        omega = sum_tiles(
             labels.reshape(devices, LANES),
             one.reshape(devices, *part),
             two.reshape(devices, *part),
             devices,
         )
-
-    omega = lax.cond(jnp.any(labels[:, 2] > 0), sum_dense, sum_shared)
-    by_dev = ((3, 0, 1, 2), (3, 0, 1, 2))
-    (partner,) = exchange(
-        [omega.reshape(SIDE, SIDE, 2, n_grp, *part)], [by_dev], 2, "send_tiles"
-    )
-    sym = symmetrize(omega, partner.reshape(omega.shape), n_grp)
+        omega = omega.reshape(SIDE, SIDE, 2, n_grp, *part).transpose(2, 3, 0, 1, 4, 5, 6)
+        (partner,) = exchange([omega], [moved], 2, "send_tiles")
+        return symmetrize(omega, partner)
+
+    sym = lax.cond(flag[0] > 0, dense, main)
     return sym.reshape(devices // n_grp, bands, n_grp, 1, bands)
 
 

time: 163 us -> 158 us (0.969)
  Pallas kernels: 158 us -> 154 us
    pallas_call x4 -> x2, Pallas kernels: 152 us -> 149 us  [the longest x1 143 us: sums_and_partners(): pl.pallas_call(main_kernel, name='sums_and_partners', out_shape=[jax.Shap...]
where the time goes in v5:
time: 158 us; the launch traced here: 155 us
  Pallas kernels  154 us (97%)
    pallas_call x1, Pallas kernels, sums_and_partners(): pl.pallas_call(main_kernel, name='sums_and_partners', out_shape=[jax.Shap...  143 us
    pallas_call x1, Pallas kernels, symmetrize(): pl.pallas_call(symmetrize_kernel, name='symmetrize', grid=(SIDE,), out_sh...  6.22 us
    pallas_call x1, Pallas kernels, make_plan(): pl.pallas_call(functools.partial(plan_kernel, grid), name='plan', out_sha...  4.88 us

profile of v5, /device:TPU:11, one launch (start us, length us, event | category | flops | bytes accessed | tf_op | source)
XLA Modules:
  0.0 155.4 jit_solution(10305373712707782249)
XLA Ops:
  0.0 0.0 copy-start.2
  0.0 0.0 copy-start.1
  0.0 0.0 copy-start
  0.7 4.9 %plan.1 = (s32[192]{0:T(256)}, s32[192]{0:T(256)}, s32[3,128]{1,0:T(4,128)}) custom-call(s32[128]{0:T(128)} %bitcast.35, s32[128]{0:T(128)} %tile.1, s32[1]{0:T(128)S(6)} %copy.17.live), custom_call_target="tpu_custom_call" | custom-call | tf_op jit(solution)/shard_map/plan/pallas_call | solution.py:222
  5.6 142.8 %sums_and_partners.1 = (bf16[2,4,4,4,3,40,128]{6,5,4,3,2,1,0:T(8,128)(2,1)S(1)}, bf16[4,4,4,2,3,40,128]{6,5,4,3,2,1,0:T(8,128)(2,1)}, s32[1]{0:T(128)}) custom-call(s32[192]{0:T(256)} %get-tuple-element.41.cell, s32[192]{0:T(256)} %get-tuple-element.42.turn, s32[3,128]{1,0:T(4,128)} %get-tuple-element.43.names, bf16[2,120,120,128]{3,2,1,0:T(8,128)(2,1)} %bitcast.22, ...), custom_call_target="tpu_custom_call" | custom-call | tf_op jit(solution)/shard_map/sums_and_partners/pallas_call | solution.py:732
  149.1 0.0 copy-done.2
  149.1 0.0 copy-done.1
  149.2 0.0 copy-done
  149.2 6.2 %conditional.1 = (f32[32,120,4,1,120]{4,3,2,1,0:T(1,128)}) conditional(s32[]{:T(128)} %bitcast.17, (bf16[2,4,4,4,3,40,128]{6,5,4,3,2,1,0:T(8,128)(2,1)S(1)}, bf16[4,4,4,2,3,40,128]{6,5,4,3,2,1,0:T(8,128)(2,1)}) %tuple.13, (s32[128]{0:T(128)S(1)}, s32[128]{0:T(128)S(1)}, s32[1]{0:T(128)}, bf16[2,120,120,128]{3,2,1,0:T(8,128)(2,1)}, ...), branch_computations={%region_0.0_spmd, %region_1.0_spmd} | conditional | bytes 23592968 | solution.py:894
  149.2 6.2 %symmetrize.2 = f32[32,480,120]{2,1,0:T(8,128)} custom-call(bf16[2,4,4,4,3,40,128]{6,5,4,3,2,1,0:T(8,128)(2,1)S(1)} %get-tuple-element.23.omega, bf16[4,4,4,2,3,40,128]{6,5,4,3,2,1,0:T(8,128)(2,1)} %get-tuple-element.24.partner), custom_call_target="tpu_custom_call" | custom-call | tf_op jit(solution)/shard_map/cond/branch_0_fun/symmetrize/pallas_call | solution.py:840
Async XLA Ops:
  0.0 149.1 %copy-start.2 = (s32[128]{0:T(128)S(1)}, s32[128]{0:T(128)}, u32[]{:S(2)}) copy-start(s32[128]{0:T(128)} %tile.1) | copy-start | bytes 1540
  0.0 149.1 %copy-start.1 = (s32[128,1]{0,1:T(1,128)S(1)}, s32[128,1]{0,1:T(1,128)}, u32[]{:S(2)}) copy-start(s32[128,1]{0,1:T(1,128)} %param.9) | copy-start | bytes 1540
  0.0 149.1 %copy-start = (f32[128,3,120]{0,2,1:T(8,128)S(1)}, f32[128,3,120]{0,2,1:T(8,128)}, u32[]{:S(2)}) copy-start(f32[128,3,120]{0,2,1:T(8,128)} %param.8) | copy-start | bytes 552964

commit v6 on v5

--- a/solution.py
+++ b/solution.py
@@ -16,6 +16,7 @@
 PARTS = 3
 WALK = 400
 PIECES = 12
+HEIGHTS = (24, 16)
 
 
 def position():
@@ -283,8 +284,7 @@
     column = line.T[0:bands]
     diff = column[:, 0:1] - line[2:3, 0:bands]
     scale = column[:, 1:2] * line[3:4, 0:bands] * jnp.exp(-diff * diff / 0.5)
-    value = jnp.pad(scale * core, ((0, 0), (0, LANES - bands)))
-    return value.reshape(PARTS, bands // PARTS, LANES).astype(jnp.bfloat16)
+    return jnp.pad(scale * core, ((0, 0), (0, LANES - bands)))
 
 
 def dense_kernel(
@@ -323,7 +323,8 @@
 
     @pl.loop(0, trip)
     def _(t):
-        block[t] = block_of(turned, rows, trip, bands, t, 0)
+        value = block_of(turned, rows, trip, bands, t, 0)
+        block[t] = value.reshape(block.shape[1:]).astype(block.dtype)
 
         @pl.when(place[t] >= 0)
         def _():
@@ -365,17 +366,20 @@
     )(owner, tile, live, strength, freqs)
 
 
-def main_kernel(
-    cell, turn, names, strength, freqs, omega_out, partner_out, flag,
-    here, turned, rows, staged, first, second, got_same, got_other, got_shared, tile_first, tile_second,
-    labels, labels_first, labels_second, labels_third, known, table, listed,
-    in_sem, send_sem, recv_sem, own_sem, last_send, last_recv, last_own, labels_send, labels_recv, labels_own,
-    tile_send, tile_recv, tile_own, small_sem,
-):
+def main_kernel(cell, turn, names, strength, freqs, *refs):
+    omega_out, partner_out, refs = refs[:2], refs[2:4], refs[4:]
+    flag, here, turned, rows, refs = *refs[:4], refs[4:]
+    staged, first, second, got_same, got_other, got_shared, tile_first, tile_second = (
+        refs[2 * r : 2 * r + 2] for r in range(8)
+    )
+    labels, labels_first, labels_second, labels_third, known, table, listed, *refs = refs[16:]
+    in_sem, send_sem, recv_sem, own_sem, last_send, last_recv, last_own, *refs = refs
+    labels_send, labels_recv, labels_own, tile_send, tile_recv, tile_own, small_sem, keep_sem = refs
     _, bands, _, trip = strength.shape
     pos = position()
     steps = (1, 3, 2)
     slabs = (1, 3, 2, 0)
+    sets = (0, 1)
     fetches = fetch_copies(strength, here, in_sem)
     for fetch in fetches:
         fetch.start()
@@ -409,81 +413,86 @@
             for u in range(8):
                 e = k * SIDE**3 + x * SIDE**2 + half * 8 + u
                 t = jnp.maximum(cell[e], 0)
-                staged[k, x, half * 2 + u // SIDE, u % SIDE] = block_of(
-                    turned, rows, trip, bands, t, turn[e]
-                )
+                value = block_of(turned, rows, trip, bands, t, turn[e])
+                begin = 0
+                for h in sets:
+                    shape = staged[h].shape[4:]
+                    end = begin + shape[0] * shape[1]
+                    staged[h][k, x, half * 2 + u // SIDE, u % SIDE] = (
+                        value[begin:end].reshape(shape).astype(staged[h].dtype)
+                    )
+                    begin = end
 
     def cut(ref, front, p, core, **at):
         index = [core] + [at.get(name, slice(None)) for name in "xyz"]
         return ref.at[(p, *index)] if front else ref.at[(*index, p)]
 
-    def early(stage, p, q):
+    def early(stage, h, p, q=None):
         axis = (p + stage) % 3
         source, target = ((staged, first), (first, second))[stage]
 
         def ends(step):
-            if axis == 0:
-                there, here_at = {"x": moved(0, step)}, {"x": pos[0]}
-            else:
-                r = slabs[q]
-                x = moved(0, (SIDE - r) % SIDE if p == 0 else r)
-                there = {"x": x, "xyz"[axis]: moved(axis, step)}
-                here_at = {"x": x, "xyz"[axis]: pos[axis]}
+            there, here_at = {"xyz"[axis]: moved(axis, step)}, {"xyz"[axis]: pos[axis]}
+            if axis and q is not None:
+                there["x"] = here_at["x"] = moved(0, slabs[q])
             return (
-                cut(source, stage > 0, p, slice(None), **there),
-                cut(target, True, p, slice(None), **here_at),
+                cut(source[h], stage > 0, p, slice(None), **there),
+                cut(target[h], True, p, slice(None), **here_at),
             )
 
         def remote(m, step):
             source_at, target_at = ends(step)
+            at = (stage, h, p, q or 0, m)
             return pltpu.make_async_remote_copy(
                 src_ref=source_at,
                 dst_ref=target_at,
-                send_sem=send_sem.at[stage, p, q, m],
-                recv_sem=recv_sem.at[stage, p, q, m],
+                send_sem=send_sem.at[at],
+                recv_sem=recv_sem.at[at],
                 device_id=device_at(pos, axis, step, False),
                 device_id_type=MESH,
             )
 
-        def local():
-            return pltpu.make_async_copy(*ends(0), own_sem.at[stage, p, q])
-
-        if axis == 0:
-            return ([remote(0, slabs[q])], []) if slabs[q] else ([], [local()])
-        return [remote(m, step) for m, step in enumerate(steps)], [local()]
-
-    def late(p, f, m):
+        local = [pltpu.make_async_copy(*ends(0), own_sem.at[stage, h, p, q or 0])]
+        if axis == 0 and q is not None:
+            return ([remote(0, slabs[q])], []) if slabs[q] else ([], local)
+        return [remote(m, step) for m, step in enumerate(steps)], local
+
+    def late(h, p, f):
         axis = (p + 2) % 3
-        step = (*steps, 0)[m]
         core = (pos[3], 1 - pos[3], 2)[f]
-        there, here_at = {"xyz"[axis]: moved(axis, step)}, {"xyz"[axis]: pos[axis]}
-        source = cut(second, True, p, core, **there)
-        index = [here_at.get(name, slice(None)) for name in "xyz"]
-        if f < 2:
-            target = (got_same, got_other)[f].at[(*index, p)]
-        else:
-            target = got_shared.at[(*index, pos[3], p)]
-        if step == 0 and f != 1:
-            return pltpu.make_async_copy(source, target, last_own.at[p, f])
-        return pltpu.make_async_remote_copy(
-            src_ref=source,
-            dst_ref=target,
-            send_sem=last_send.at[p, f, m],
-            recv_sem=last_recv.at[p, f, m],
-            device_id=device_at(pos, axis, step, f == 1),
-            device_id_type=MESH,
-        )
-
-    def is_local(f, m):
-        return m == 3 and f != 1
-
-    def pass_on(p):
-        mine = got_shared.at[:, :, :, pos[3], p]
+
+        def ends(step):
+            source = cut(second[h], True, p, core, **{"xyz"[axis]: moved(axis, step)})
+            index = [slice(None)] * 3
+            index[axis] = pos[axis]
+            if f == 2:
+                return source, got_shared[h].at[(*index, pos[3], p)]
+            return source, (got_same, got_other)[f][h].at[(*index, p)]
+
+        remotes = []
+        for m, step in enumerate((*steps, 0) if f == 1 else steps):
+            source, target = ends(step)
+            remotes.append(
+                pltpu.make_async_remote_copy(
+                    src_ref=source,
+                    dst_ref=target,
+                    send_sem=last_send.at[h, p, f, m],
+                    recv_sem=last_recv.at[h, p, f, m],
+                    device_id=device_at(pos, axis, step, f == 1),
+                    device_id_type=MESH,
+                )
+            )
+        if f == 1:
+            return remotes, []
+        return remotes, [pltpu.make_async_copy(*ends(0), last_own.at[h, p, f])]
+
+    def pass_on(h, p):
+        mine = got_shared[h].at[:, :, :, pos[3], p]
         return pltpu.make_async_remote_copy(
             src_ref=mine,
             dst_ref=mine,
-            send_sem=last_send.at[p, 3, 0],
-            recv_sem=last_recv.at[p, 3, 0],
+            send_sem=last_send.at[h, p, 3, 0],
+            recv_sem=last_recv.at[h, p, 3, 0],
             device_id=device_at(pos, 0, 0, True),
             device_id_type=MESH,
         )
@@ -581,9 +590,11 @@
         copy.wait()
 
     n_slots = 4 * SIDE**3
-    sums = turned.reshape(n_slots + 1, PARTS, bands // PARTS, LANES)
-
-    def sum_group(got, begin, end):
+    sums = turned.reshape(n_slots + 1, bands // 8, 8, LANES)
+    tile_rows = [staged[h].shape[4] * staged[h].shape[5] // 8 for h in sets]
+    spans = [slice(0, tile_rows[0]), slice(tile_rows[0], sum(tile_rows))]
+
+    def sum_group(h, got, begin, end):
         def add(r, total):
             kept = listed[1, r].astype(jnp.float32)
             at = listed[0, r]
@@ -591,166 +602,173 @@
             for length in reversed(got.shape[:-3]):
                 index.insert(0, jnp.bitwise_and(at, length - 1))
                 at = lax.shift_right_logical(at, length.bit_length() - 1)
-            total = total * kept + got[tuple(index)].astype(jnp.float32)
-            sums[r] = total
+            block = got[tuple(index)].astype(jnp.float32).reshape(total.shape)
+            total = total * kept + block
+            sums[r, spans[h]] = total
             return total
 
-        lax.fori_loop(begin, end, add, jnp.zeros(sums.shape[1:], jnp.float32), unroll=4)
-
-    def sum_part(p):
+        lax.fori_loop(
+            begin, end, add, jnp.zeros((tile_rows[h], 8, LANES), jnp.float32), unroll=4
+        )
+
+    def sum_part(h, p):
+        _, height, _ = staged[h].shape[4:]
+        begin = spans[h].start + p * height // 8
+        span = slice(begin, begin + height // 8)
+
         @pl.loop(0, n_slots // 2, unroll=8)
         def _(k):
-            total = sums[listed[2, k], p] + sums[listed[3, k], p] + sums[listed[4, k], p]
+            total = sums[listed[2, k]][span] + sums[listed[3, k]][span] + sums[listed[4, k]][span]
             x, d = lax.rem(k, SIDE), lax.div(k, SIDE)
-            staged[lax.rem(d, 2), x, lax.div(d, 8), lax.rem(lax.div(d, 2), SIDE), p] = (
-                total.astype(staged.dtype)
+            staged[h][lax.rem(d, 2), x, lax.div(d, 8), lax.rem(lax.div(d, 2), SIDE), p] = (
+                total.reshape(height, LANES).astype(staged[h].dtype)
             )
 
-    def tile_messages(stage, p, f):
+    def tile_messages(stage, h, p, f=None):
         axis = (p + stage) % 3
-        core = 1 - pos[3] if f else pos[3]
+        core = slice(0, 2) if f is None else (1 - pos[3] if f else pos[3])
 
         def ends(step):
             there, here_at = {"xyz"[axis]: moved(axis, step)}, {"xyz"[axis]: pos[axis]}
-            source = cut((staged, tile_first, tile_second)[stage], stage > 0, p, core, **there)
+            source = cut((staged, tile_first, tile_second)[stage][h], stage > 0, p, core, **there)
             if stage < 2:
-                return source, cut((tile_first, tile_second)[stage], True, p, core, **here_at)
+                return source, cut((tile_first, tile_second)[stage][h], True, p, core, **here_at)
             index = [here_at.get(name, slice(None)) for name in "xyz"]
-            return source, partner_out.at[(*index, pos[3], p)]
-
-        crossing = stage == 2 and f == 1
+            return source, partner_out[h].at[(*index, pos[3], p)]
+
         remotes = []
-        for m, step in enumerate((*steps, 0) if crossing else steps):
+        for m, step in enumerate((*steps, 0) if f else steps):
             source, target = ends(step)
+            at = (stage, h, p, f or 0, m)
             remotes.append(
                 pltpu.make_async_remote_copy(
                     src_ref=source,
                     dst_ref=target,
-                    send_sem=tile_send.at[stage, p, f, m],
-                    recv_sem=tile_recv.at[stage, p, f, m],
-                    device_id=device_at(pos, axis, step, crossing),
+                    send_sem=tile_send.at[at],
+                    recv_sem=tile_recv.at[at],
+                    device_id=device_at(pos, axis, step, bool(f)),
                     device_id_type=MESH,
                 )
             )
-        if crossing:
+        if f:
             return remotes, []
-        return remotes, [pltpu.make_async_copy(*ends(0), tile_own.at[stage, p, f])]
+        return remotes, [pltpu.make_async_copy(*ends(0), tile_own.at[stage, h, p])]
 
     start(label_messages(0))
     for q in range(SIDE):
         compute(moved(0, slabs[q]))
         for p in range(PARTS):
-            start(early(0, p, q))
+            start(early(0, 0, p, q))
+    for p in range(PARTS):
+        start(early(0, 1, p))
     arrive(label_messages(0))
     start(label_messages(1))
-    for q in range(SIDE):
-        for p in range(PARTS):
-            arrive(early(0, p, q))
-            start(early(1, p, q))
+    for p in range(PARTS):
+        for q in range(SIDE):
+            remotes, local = early(0, 0, p, q)
+            arrive((remotes, local))
+        start(early(1, 0, p))
+    for p in range(PARTS):
+        arrive(early(0, 1, p))
+        start(early(1, 1, p))
     arrive(label_messages(1))
     start(label_messages(2))
-    for q in range(SIDE):
-        arrive(early(1, 1, q))
-        m = (*steps, 0).index(slabs[q])
-        for f in (2, 1, 0):
-            late(1, f, m).start()
-    for p in (0, 2):
-        for q in range(SIDE):
-            arrive(early(1, p, q))
-        for f in (2, 1, 0):
-            for m in range(4):
-                late(p, f, m).start()
+    for h in sets:
+        for p in range(PARTS):
+            arrive(early(1, h, p))
+            for f in (2, 1, 0):
+                start(late(h, p, f))
     arrive(label_messages(2))
     order_labels()
     sums[n_slots] = jnp.zeros(sums.shape[1:], jnp.float32)
-
-    def arrive_late(p, f):
-        for m in range(4):
-            if is_local(f, m):
-                late(p, f, m).wait()
-            else:
-                late(p, f, m).wait_recv()
-
-    for p in (1, 0, 2):
-        arrive_late(p, 2)
-        pass_on(p).start()
-    for p in (1, 0, 2):
-        arrive_late(p, 1)
-    sum_group(got_other, n_slots // 2, n_slots * 3 // 4)
-    for p in (1, 0, 2):
-        pass_on(p).wait_recv()
-    sum_group(got_shared, 0, n_slots // 2)
-    for stage in range(2):
-        for p in range(PARTS):
-            for q in range(SIDE):
-                for copy in early(stage, p, q)[0]:
+    keeps = [
+        pltpu.make_async_copy(staged[h].at[0:2], omega_out[h], keep_sem.at[h]) for h in sets
+    ]
+    for h in sets:
+        for p in range(PARTS):
+            arrive(late(h, p, 2))
+            pass_on(h, p).start()
+        for p in range(PARTS):
+            arrive(late(h, p, 1))
+        sum_group(h, got_other[h], n_slots // 2, n_slots * 3 // 4)
+        for p in range(PARTS):
+            pass_on(h, p).wait_recv()
+        sum_group(h, got_shared[h], 0, n_slots // 2)
+        for p in range(PARTS):
+            for q in [None] if h else range(SIDE):
+                for copy in early(0, h, p, q)[0]:
                     copy.wait_send()
-    for p in (1, 0, 2):
-        arrive_late(p, 0)
-    sum_group(got_same, n_slots * 3 // 4, n_slots)
-    tile_jobs = [(p, f) for p in (1, 0, 2) for f in (1, 0)]
-    for p in (1, 0, 2):
-        sum_part(p)
-        for f in (1, 0):
-            start(tile_messages(0, p, f))
-    keep = pltpu.make_async_copy(staged.at[0:2], omega_out, small_sem)
-    keep.start()
-    for stage in (1, 2):
-        for job in tile_jobs:
-            arrive(tile_messages(stage - 1, *job))
-            start(tile_messages(stage, *job))
-    for p in range(PARTS):
-        pass_on(p).wait_send()
-        for f in range(3):
-            for m in range(4):
-                if not is_local(f, m):
-                    late(p, f, m).wait_send()
+        for p in range(PARTS):
+            arrive(late(h, p, 0))
+        sum_group(h, got_same[h], n_slots * 3 // 4, n_slots)
+        for p in range(PARTS):
+            sum_part(h, p)
+            start(tile_messages(0, h, p))
+        keeps[h].start()
+    for h in sets:
+        for p in range(PARTS):
+            arrive(tile_messages(0, h, p))
+            start(tile_messages(1, h, p))
+    for h in sets:
+        for p in range(PARTS):
+            arrive(tile_messages(1, h, p))
+            for f in (1, 0):
+                start(tile_messages(2, h, p, f))
+    for h in sets:
+        for p in range(PARTS):
+            pass_on(h, p).wait_send()
+            sent = [early(1, h, p)] + [late(h, p, f) for f in range(3)]
+            sent += [tile_messages(0, h, p), tile_messages(1, h, p)]
+            for remotes, _ in sent:
+                for copy in remotes:
+                    copy.wait_send()
     for stage in range(3):
         for copy in label_messages(stage)[0]:
             copy.wait_send()
-    for job in tile_jobs:
-        arrive(tile_messages(2, *job))
-    keep.wait()
-    for stage in range(3):
-        for job in tile_jobs:
-            for copy in tile_messages(stage, *job)[0]:
-                copy.wait_send()
+    for h in sets:
+        keeps[h].wait()
+        for p in range(PARTS):
+            for f in (1, 0):
+                arrive(tile_messages(2, h, p, f))
+    for h in sets:
+        for p in range(PARTS):
+            for f in (1, 0):
+                for copy in tile_messages(2, h, p, f)[0]:
+                    copy.wait_send()
 
 
 def sums_and_partners(cell, turn, labels, strength, freqs, collective_id):
     _, bands, _, trip = strength.shape
-    part = (bands // PARTS, LANES)
     torus = (SIDE, SIDE, SIDE)
-    moving = pltpu.VMEM((PARTS, 3, *torus, *part), jnp.bfloat16)
-    moving_tiles = pltpu.VMEM((PARTS, 2, *torus, *part), jnp.bfloat16)
     smem = pl.BlockSpec(memory_space=pltpu.SMEM)
     anywhere = pl.BlockSpec(memory_space=pl.ANY)
     label_rows = (*torus, 2, 1, 1, LANES)
     moving_labels = pltpu.VMEM(label_rows, jnp.int32)
     dma = pltpu.SemaphoreType.DMA
     slots = 4 * SIDE**3
+    parts = [(PARTS, height, LANES) for height in HEIGHTS]
+
+    def both(*front):
+        return [(*front, *part) for part in parts]
+
+    def moving(cores):
+        return [(PARTS, cores, *torus, *part[1:]) for part in parts]
+
+    buffers = [both(3, *torus), moving(3), moving(3), both(*torus), both(*torus), both(*torus, 2)]
+    buffers += [moving(2), moving(2)]
+    outs = both(2, *torus) + both(*torus, 2)
     return pl.pallas_call(
         main_kernel,
         name="sums_and_partners",
-        out_shape=[
-            jax.ShapeDtypeStruct((2, *torus, PARTS, *part), jnp.bfloat16),
-            jax.ShapeDtypeStruct((*torus, 2, PARTS, *part), jnp.bfloat16),
-            jax.ShapeDtypeStruct((1,), jnp.int32),
-        ],
+        out_shape=[jax.ShapeDtypeStruct(shape, jnp.bfloat16) for shape in outs]
+        + [jax.ShapeDtypeStruct((1,), jnp.int32)],
         in_specs=[smem, smem, smem, anywhere, pl.BlockSpec(memory_space=pltpu.VMEM)],
-        out_specs=[anywhere, anywhere, smem],
+        out_specs=[anywhere] * 4 + [smem],
         scratch_shapes=[
             pltpu.VMEM(strength.shape, strength.dtype),
             pltpu.VMEM((2 * trip + 1, bands, LANES), jnp.float32),
             pltpu.VMEM((2 * trip, 8, LANES), jnp.float32),
-            pltpu.VMEM((3, *torus, PARTS, *part), jnp.bfloat16),
-            moving,
-            moving,
-            pltpu.VMEM((*torus, PARTS, *part), jnp.bfloat16),
-            pltpu.VMEM((*torus, PARTS, *part), jnp.bfloat16),
-            pltpu.VMEM((*torus, 2, PARTS, *part), jnp.bfloat16),
-            moving_tiles,
-            moving_tiles,
+            *[pltpu.VMEM(shape, jnp.bfloat16) for pair in buffers for shape in pair],
             moving_labels,
             moving_labels,
             moving_labels,
@@ -759,19 +777,20 @@
             pltpu.VMEM((8, slots), jnp.int32),
             pltpu.SMEM((8, slots), jnp.int32),
             dma((PIECES,)),
-            dma((2, PARTS, SIDE, 3)),
-            dma((2, PARTS, SIDE, 3)),
-            dma((2, PARTS, SIDE)),
-            dma((PARTS, 4, 4)),
-            dma((PARTS, 4, 4)),
-            dma((PARTS, 3)),
+            dma((2, 2, PARTS, SIDE, 3)),
+            dma((2, 2, PARTS, SIDE, 3)),
+            dma((2, 2, PARTS, SIDE)),
+            dma((2, PARTS, 4, 4)),
+            dma((2, PARTS, 4, 4)),
+            dma((2, PARTS, 3)),
             dma((3, 7)),
             dma((3, 7)),
             dma((3,)),
-            dma((3, PARTS, 2, 4)),
-            dma((3, PARTS, 2, 4)),
-            dma((3, PARTS, 2)),
+            dma((3, 2, PARTS, 2, 4)),
+            dma((3, 2, PARTS, 2, 4)),
+            dma((3, 2, PARTS)),
             dma,
+            dma((2,)),
         ],
         compiler_params=pltpu.CompilerParams(
             collective_id=collective_id, has_side_effects=True, vmem_limit_bytes=60 * 2**20
@@ -819,36 +838,44 @@
     )(labels, one, two)
 
 
-def symmetrize_kernel(omega, partner, out):
-    *_, thirds, part, lanes = omega.shape
-    bands = thirds * part
+def symmetrize_kernel(n, *refs):
+    omegas, partners, out = refs[:n], refs[n : 2 * n], refs[2 * n]
+    bands = out.shape[2]
+
+    def whole(refs, at):
+        pieces = [ref[at].astype(jnp.float32).reshape(-1, LANES) for ref in refs]
+        return jnp.concatenate(pieces, axis=0)
+
     for z in range(SIDE):
         for core in range(2):
             for x in range(SIDE):
-                mine = omega[core, x, 0, z].astype(jnp.float32).reshape(bands, lanes)
-                other = partner[x, 0, z, core].astype(jnp.float32).reshape(bands, lanes).T
+                mine = whole(omegas, (core, x, 0, z))
+                other = whole(partners, (x, 0, z, core)).T
                 out[z * 2 + core, pl.ds(x, bands, stride=SIDE), :] = 0.5 * (
                     mine[:, 0:bands] + other[0:bands]
                 )
 
 
-def symmetrize(omega, partner):
-    *_, thirds, part, lanes = omega.shape
-    bands = thirds * part
-    rest = (thirds, part, lanes)
+def symmetrize(omegas, partners):
+    rests = [omega.shape[4:] for omega in omegas]
+    bands = sum(rest[0] * rest[1] for rest in rests)
     rows = 2 * SIDE
     return pl.pallas_call(
-        symmetrize_kernel,
+        functools.partial(symmetrize_kernel, len(omegas)),
         name="symmetrize",
         grid=(SIDE,),
         out_shape=jax.ShapeDtypeStruct((rows * SIDE, bands * SIDE, bands), jnp.float32),
         in_specs=[
-            pl.BlockSpec((2, SIDE, 1, SIDE, *rest), lambda y: (0, 0, y, 0, 0, 0, 0)),
-            pl.BlockSpec((SIDE, 1, SIDE, 2, *rest), lambda y: (0, y, 0, 0, 0, 0, 0)),
+            pl.BlockSpec((2, SIDE, 1, SIDE, *rest), lambda y: (0, 0, y, 0, 0, 0, 0))
+            for rest in rests
+        ]
+        + [
+            pl.BlockSpec((SIDE, 1, SIDE, 2, *rest), lambda y: (0, y, 0, 0, 0, 0, 0))
+            for rest in rests
         ],
         out_specs=pl.BlockSpec((rows, bands * SIDE, bands), lambda y: (y, 0, 0)),
         compiler_params=pltpu.CompilerParams(vmem_limit_bytes=60 * 2**20),
-    )(omega, partner)
+    )(*omegas, *partners)
 
 
 def per_device(strength, freqs, owner, tile_slot, live_count):
@@ -867,12 +894,12 @@
         return labels.reshape(*torus, 2, 1, 1, LANES)
 
     cell, turn, labels = make_plan(*names, grid)
-    omega, partner, flag = sums_and_partners(
+    *halves, flag = sums_and_partners(
         cell, turn, labels, by_lane, freqs, 1
     )
 
     def main():
-        return symmetrize(omega, partner)
+        return symmetrize(halves[:2], halves[2:])
 
     def dense():
         cells, labels = dense_blocks(by_lane, freqs, *names, grid)
@@ -889,7 +916,7 @@
         )
         omega = omega.reshape(SIDE, SIDE, 2, n_grp, *part).transpose(2, 3, 0, 1, 4, 5, 6)
         (partner,) = exchange([omega], [moved], 2, "send_tiles")
-        return symmetrize(omega, partner)
+        return symmetrize([omega], [partner])
 
     sym = lax.cond(flag[0] > 0, dense, main)
     return sym.reshape(devices // n_grp, bands, n_grp, 1, bands)

time: 158 us -> 150 us (0.949); the launches traced: 155 us -> 149 us
  Pallas kernels: 154 us -> 148 us
    pallas_call x1, Pallas kernels: 143 us -> 139 us  [sums_and_partners(): pl.pallas_call(main_kernel, name='sums_and_partners', out_shape=[jax.Shap...]
    pallas_call x1, Pallas kernels: 4.88 us -> 2.86 us  [make_plan(): pl.pallas_call(functools.partial(plan_kernel, grid), name='plan', out_sha...]
where the time goes in v6:
time: 150 us; the launch traced here: 149 us
  Pallas kernels  148 us (99%)
    pallas_call x1, Pallas kernels, sums_and_partners(): pl.pallas_call(main_kernel, name='sums_and_partners', out_shape=[jax.Shap...  139 us
    pallas_call x1, Pallas kernels, symmetrize(): pl.pallas_call(functools.partial(symmetrize_kernel, len(omegas)), name='s...  6.17 us

profile of v6, /device:TPU:11, one launch (start us, length us, event | category | flops | bytes accessed | tf_op | source)
XLA Modules:
  0.0 149.1 jit_solution(14351239028912849302)
XLA Ops:
  0.0 0.0 copy-start.2
  0.0 0.0 copy-start.1
  0.0 0.0 copy-start
  0.7 2.9 %plan.1 = (s32[192]{0:T(256)}, s32[192]{0:T(256)}, s32[3,128]{1,0:T(4,128)}) custom-call(s32[128]{0:T(128)} %bitcast.35, s32[128]{0:T(128)} %tile.1, s32[1]{0:T(128)S(6)} %copy.17.live), custom_call_target="tpu_custom_call" | custom-call | tf_op jit(solution)/shard_map/plan/pallas_call | solution.py:223
  3.6 138.7 %sums_and_partners.1 = (bf16[2,4,4,4,3,24,128]{6,5,4,3,2,1,0:T(8,128)(2,1)S(1)}, bf16[2,4,4,4,3,16,128]{6,5,4,3,2,1,0:T(8,128)(2,1)S(1)}, bf16[4,4,4,2,3,24,128]...) custom-call(s32[192]{0:T(256)} %get-tuple-element.49.cell, s32[192]{0:T(256)} %get-tuple-element.50.turn, ...), custom_call_target="tpu_custom_call" | custom-call | tf_op jit(solution)/shard_map/sums_and_partners/pallas_call | solution.py:760
  142.9 0.0 copy-done.2
  142.9 0.0 copy-done.1
  143.0 0.0 copy-done
  143.0 6.2 %conditional.1 = (f32[32,120,4,1,120]{4,3,2,1,0:T(1,128)}) conditional(s32[]{:T(128)} %bitcast.17, (bf16[2,4,4,4,3,24,128]{6,5,4,3,2,1,0:T(8,128)(2,1)S(1)}, bf16[2,4,4,4,3,16,128]{6,5,4,3,2,1,0:T(8,128)(2,1)S(1)}, bf16[4,4,4,2,3,24,128]{6,5,4,3,2,1,0:T(8,128)(2,1)}, bf16[4,4,4,2,3,16,128]{6,5,4,3,2,1,0:T(8,128)(2,1)}) %tuple.13, (s32[128]{0:T(128)S(1)}, ...), branch_computations={%region_0.0_spmd, %region_1.0_spmd} | conditional | bytes 23592968 | solution.py:921
  143.0 6.2 %symmetrize.2 = f32[32,480,120]{2,1,0:T(8,128)} custom-call(bf16[2,4,4,4,3,24,128]{6,5,4,3,2,1,0:T(8,128)(2,1)S(1)} %get-tuple-element.27.refs_0_, bf16[2,4,4,4,3,16,128]{6,5,4,3,2,1,0:T(8,128)(2,1)S(1)} %get-tuple-element.28.refs_1_, bf16[4,4,4,2,3,24,128]{6,5,4,3,2,1,0:T(8,128)(2,1)} %get-tuple-element.29.refs_2_, ...), custom_call_target="tpu_custom_call" | custom-call | tf_op jit(solution)/shard_map/cond/branch_0_fun/symmetrize/pallas_call | solution.py:863
Async XLA Ops:
  0.0 142.9 %copy-start.2 = (s32[128]{0:T(128)S(1)}, s32[128]{0:T(128)}, u32[]{:S(2)}) copy-start(s32[128]{0:T(128)} %tile.1) | copy-start | bytes 1540
  0.0 142.9 %copy-start.1 = (s32[128,1]{0,1:T(1,128)S(1)}, s32[128,1]{0,1:T(1,128)}, u32[]{:S(2)}) copy-start(s32[128,1]{0,1:T(1,128)} %param.9) | copy-start | bytes 1540
  0.0 142.9 %copy-start = (f32[128,3,120]{0,2,1:T(8,128)S(1)}, f32[128,3,120]{0,2,1:T(8,128)}, u32[]{:S(2)}) copy-start(f32[128,3,120]{0,2,1:T(8,128)} %param.8) | copy-start | bytes 552964

commit v7 on v6

--- a/solution.py
+++ b/solution.py
@@ -167,13 +167,15 @@
         o = owner[t]
         e = lax.rem(o, 2) * chips + lax.div(o, 2)
         held = cell[e]
+        alive = t < live[0]
         taken = held >= 0
-        cell[e] = jnp.where(taken, held, t)
-        labels[0, o] = jnp.where(taken, labels[0, o], tile[t])
+        kept = taken | jnp.logical_not(alive)
+        cell[e] = jnp.where(kept, held, t)
+        labels[0, o] = jnp.where(kept, labels[0, o], tile[t])
         left[n] = t
-        return n + taken.astype(jnp.int32)
-
-    n_left = lax.fori_loop(0, live[0], first, jnp.int32(0))
+        return n + (taken & alive).astype(jnp.int32)
+
+    n_left = lax.fori_loop(0, tile.shape[0], first, jnp.int32(0), unroll=8)
 
     def insert(q, carry):
         lost, noise = carry
@@ -676,7 +678,9 @@
     for h in sets:
         for p in range(PARTS):
             arrive(early(1, h, p))
-            for f in (2, 1, 0):
+            start(late(h, p, 2))
+        for f in (1, 0):
+            for p in range(PARTS):
                 start(late(h, p, f))
     arrive(label_messages(2))
     order_labels()

time: 150 us -> 148 us (0.987)
    pallas_call x1, Pallas kernels: 139 us -> 137 us  [sums_and_partners(): pl.pallas_call(main_kernel, name='sums_and_partners', out_shape=[jax.Shap...]
where the time goes in v7:
time: 148 us
  Pallas kernels  147 us (99%)
    pallas_call x1, Pallas kernels, sums_and_partners(): pl.pallas_call(main_kernel, name='sums_and_partners', out_shape=[jax.Shap...  137 us
    pallas_call x1, Pallas kernels, symmetrize(): pl.pallas_call(functools.partial(symmetrize_kernel, len(omegas)), name='s...  6.17 us
    pallas_call x1, Pallas kernels, make_plan(): pl.pallas_call(functools.partial(plan_kernel, grid), name='plan', out_sha...  3.74 us

profile of v7, /device:TPU:11, one launch (start us, length us, event | category | flops | bytes accessed | tf_op | source)
XLA Modules:
  0.0 148.2 jit_solution(5633797340907431877)
XLA Ops:
  0.0 0.0 copy-start.2
  0.0 0.0 copy-start.1
  0.0 0.0 copy-start
  0.7 3.7 %plan.1 = (s32[192]{0:T(256)}, s32[192]{0:T(256)}, s32[3,128]{1,0:T(4,128)}) custom-call(s32[128]{0:T(128)} %bitcast.35, s32[128]{0:T(128)} %tile.1, s32[1]{0:T(128)S(6)} %copy.17.live), custom_call_target="tpu_custom_call" | custom-call | tf_op jit(solution)/shard_map/plan/pallas_call | solution.py:225
  4.4 136.9 %sums_and_partners.1 = (bf16[2,4,4,4,3,24,128]{6,5,4,3,2,1,0:T(8,128)(2,1)S(1)}, bf16[2,4,4,4,3,16,128]{6,5,4,3,2,1,0:T(8,128)(2,1)S(1)}, bf16[4,4,4,2,3,24,128]...) custom-call(s32[192]{0:T(256)} %get-tuple-element.49.cell, s32[192]{0:T(256)} %get-tuple-element.50.turn, ...), custom_call_target="tpu_custom_call" | custom-call | tf_op jit(solution)/shard_map/sums_and_partners/pallas_call | solution.py:764
  142.0 0.0 copy-done.2
  142.0 0.0 copy-done.1
  142.0 0.0 copy-done
  142.1 6.2 %conditional.1 = (f32[32,120,4,1,120]{4,3,2,1,0:T(1,128)}) conditional(s32[]{:T(128)} %bitcast.17, (bf16[2,4,4,4,3,24,128]{6,5,4,3,2,1,0:T(8,128)(2,1)S(1)}, bf16[2,4,4,4,3,16,128]{6,5,4,3,2,1,0:T(8,128)(2,1)S(1)}, bf16[4,4,4,2,3,24,128]{6,5,4,3,2,1,0:T(8,128)(2,1)}, bf16[4,4,4,2,3,16,128]{6,5,4,3,2,1,0:T(8,128)(2,1)}) %tuple.13, (s32[128]{0:T(128)S(1)}, ...), branch_computations={%region_0.0_spmd, %region_1.0_spmd} | conditional | bytes 23592968 | solution.py:925
  142.1 6.2 %symmetrize.2 = f32[32,480,120]{2,1,0:T(8,128)} custom-call(bf16[2,4,4,4,3,24,128]{6,5,4,3,2,1,0:T(8,128)(2,1)S(1)} %get-tuple-element.27.refs_0_, bf16[2,4,4,4,3,16,128]{6,5,4,3,2,1,0:T(8,128)(2,1)S(1)} %get-tuple-element.28.refs_1_, bf16[4,4,4,2,3,24,128]{6,5,4,3,2,1,0:T(8,128)(2,1)} %get-tuple-element.29.refs_2_, ...), custom_call_target="tpu_custom_call" | custom-call | tf_op jit(solution)/shard_map/cond/branch_0_fun/symmetrize/pallas_call | solution.py:867
Async XLA Ops:
  0.0 142.0 %copy-start.2 = (s32[128]{0:T(128)S(1)}, s32[128]{0:T(128)}, u32[]{:S(2)}) copy-start(s32[128]{0:T(128)} %tile.1) | copy-start | bytes 1540
  0.0 142.0 %copy-start.1 = (s32[128,1]{0,1:T(1,128)S(1)}, s32[128,1]{0,1:T(1,128)}, u32[]{:S(2)}) copy-start(s32[128,1]{0,1:T(1,128)} %param.9) | copy-start | bytes 1540
  0.0 142.0 %copy-start = (f32[128,3,120]{0,2,1:T(8,128)S(1)}, f32[128,3,120]{0,2,1:T(8,128)}, u32[]{:S(2)}) copy-start(f32[128,3,120]{0,2,1:T(8,128)} %param.8) | copy-start | bytes 552964
